TPU v7x, 32 devices: a whole 2x2x4 slice. The times are simulated.
32 devices in a mesh: vox: 8 (over z, x), rep: 4 (over y, core).
Axes of the slice: x: 2, y: 2, z: 4, core: 2. Of those that a mesh axis runs over, the one named last changes fastest.
Arguments:
- fine_feats: bfloat16 [4, 32768, 192], P('rep', 'vox'), may hold values from -6 to 6
- occupancy: int32 [4, 32768], P('rep', 'vox'), may hold values 0 or 1
- parent: int32 [4, 4096], P('rep', 'vox'), may hold values from 0 to 4095, as said below
- neighbors: int32 [4, 27, 4096], P('rep', None, 'vox'), may hold values from -1 to 4095, as said below
- cotangent: bfloat16 [4, 32768, 192], P('rep', 'vox'), may hold values from -0.046875 to 0.046875
- down_weight: bfloat16 [8, 192, 192], replicated, may hold values from -0.21875 to 0.21875
- conv_weight: bfloat16 [27, 192, 192], replicated, may hold values from -0.15625 to 0.15625
- up_weight: bfloat16 [192, 8, 192], replicated, may hold values from -0.4375 to 0.4375
Outputs:
- grad_down: bfloat16 [8, 192, 192], replicated
- grad_conv: bfloat16 [27, 192, 192], replicated
- grad_up: bfloat16 [192, 8, 192], replicated
Inputs may be any that keep to these rules, and one draw needn't show every extreme that they name: Each scene's ids 0 to 4095 each appear exactly once; the parent of a group on vox index d is owned by index parent // 512; the groups of one device name at most 2 parents owned by any one other device, and in every draw some device names exactly 2 at some other device. `neighbors`: entry 13 is the coarse voxel itself; every present neighbor is owned by the same vox index or one of the two next to it.
All inputs are finite; a program needn't handle non-finite values. No bound on the sum of `occupancy` on one device may be relied on, other than what follows from the above.
Results may differ from a plain program's by a relative error of at most 0.0095.
Values may be sent and summed in bfloat16 or wider, within the bound.
A program may use at most 128 MiB of HBM per device.

v0:
```python
import jax
import jax.numpy as jnp
from jax import lax
from jax.sharding import PartitionSpec as P

CAP = 2


def with_halo(array, sides, width):
    for axis, dim in sides:
        peers, length = (lax.axis_size(axis), array.shape[dim])
        up = [(i, (i + 1) % peers) for i in range(peers - 1)]
        down = [(j, i) for i, j in up]
        last = lax.slice_in_dim(array, length - width, length, axis=dim)
        initial = lax.slice_in_dim(array, 0, width, axis=dim)
        before = lax.ppermute(last, axis, up)
        after = lax.ppermute(initial, axis, down)
        array = jnp.concatenate([before, array, after], axis=dim)
    return array


def passed_along(block, axis, distance):
    devices = range(lax.axis_size(axis))
    route = [(i - distance, i) for i in devices if i - distance in devices]
    return lax.ppermute(block, axis, route)


def contract_first(left, right):
    return lax.dot_general(
        left, right, (((0,), (0,)), ((), ())), preferred_element_type=jnp.float32
    )


def contract_last(left, right):
    return lax.dot_general(
        left, right, (((1,), (1,)), ((), ())), preferred_element_type=jnp.float32
    )


def per_device(
    fine_feats, occupancy, parent, neighbors, cotangent, down_weight, conv_weight, up_weight
):
    fine_rows = fine_feats[0]
    occupied = occupancy[0]
    parents = parent[0]
    near_ids = neighbors[0]
    cot_rows = cotangent[0]
    channels = fine_rows.shape[1]
    group_count = parents.shape[0]
    vox_count = lax.axis_size("vox")
    own_index = lax.axis_index("vox")
    owner = parents // group_count
    local_id = parents % group_count
    remote = owner != own_index
    owner_hits = (
        (owner[:, None] == jnp.arange(vox_count, dtype=jnp.int32)[None, :]) & remote[:, None]
    ).astype(jnp.int32)
    ranks = jnp.cumsum(owner_hits, axis=0) - 1
    slot = jnp.sum(ranks * owner_hits, axis=1)
    dest = jnp.where(remote, owner * CAP + slot, vox_count * CAP)

    def to_coarse(values):
        send_rows = (
            jnp.zeros((vox_count * CAP, channels), jnp.float32).at[dest].set(values, mode="drop")
        )
        send_ids = jnp.full((vox_count * CAP,), -1, jnp.int32).at[dest].set(local_id, mode="drop")
        got_rows, got_ids = (
            lax.all_to_all(
                send_rows.reshape(vox_count, CAP, channels),
                "vox",
                split_axis=0,
                concat_axis=0,
                tiled=True,
            ),
            lax.all_to_all(
                send_ids.reshape(vox_count, CAP), "vox", split_axis=0, concat_axis=0, tiled=True
            ),
        )
        keep_local = jnp.where(remote, group_count, local_id)
        coarse = (
            jnp.zeros((group_count, channels), jnp.float32).at[keep_local].set(values, mode="drop")
        )
        recv_index = jnp.where(got_ids.reshape(-1) < 0, group_count, got_ids.reshape(-1))
        coarse = coarse.at[recv_index].add(got_rows.reshape(-1, channels), mode="drop")
        return (coarse, recv_index)

    def to_children(coarse_half, recv_index):
        table = jnp.concatenate([coarse_half, jnp.zeros((1, channels), jnp.bfloat16)], 0)
        outgoing = table[recv_index].reshape(vox_count, CAP, channels)
        returned = lax.all_to_all(outgoing, "vox", split_axis=0, concat_axis=0, tiled=True).reshape(
            vox_count * CAP, channels
        )
        returned = jnp.concatenate([returned, jnp.zeros((1, channels), jnp.bfloat16)], 0)
        return jnp.where(remote[:, None], returned[dest], coarse_half[local_id])

    mask_half = occupied.astype(jnp.bfloat16)[:, None]
    grouped = (fine_rows * mask_half).reshape(group_count, 8 * channels)
    pre_groups = jnp.dot(
        grouped, down_weight.reshape(8 * channels, channels), preferred_element_type=jnp.float32
    )
    pre, recv_index = to_coarse(pre_groups)
    hidden = jax.nn.silu(pre).astype(jnp.bfloat16)
    extended = with_halo(hidden, (("vox", 0),), group_count)
    extended = jnp.concatenate([extended, jnp.zeros((1, channels), jnp.bfloat16)], 0)
    ext_index = jnp.where(
        near_ids < 0,
        3 * group_count,
        (near_ids // group_count - own_index + 1) * group_count + near_ids % group_count,
    )

    def forward_offset(total, inputs):
        index_row, weight_here = inputs
        rows_here = extended[index_row]
        return (total + jnp.dot(rows_here, weight_here, preferred_element_type=jnp.float32), None)

    conv, unused_out = lax.scan(
        forward_offset, jnp.zeros((group_count, channels), jnp.float32), (ext_index, conv_weight)
    )
    upper = (hidden.astype(jnp.float32) + conv).astype(jnp.bfloat16)
    up_rows = to_children(upper, recv_index)
    cot_groups = (cot_rows * mask_half).reshape(group_count, 8 * channels)
    up_flat = up_weight.reshape(channels, 8 * channels)
    up_term = contract_first(up_rows, cot_groups)
    back_groups = contract_last(cot_groups, up_flat)
    grad_z, unused_index = to_coarse(back_groups)
    dz_half = grad_z.astype(jnp.bfloat16)

    def backward_offset(spread_now, inputs):
        index_row, weight_here = inputs
        rows_here = extended[index_row]
        term_here = contract_first(rows_here, dz_half)
        spread_now = spread_now.at[index_row].add(contract_last(dz_half, weight_here))
        return (spread_now, term_here)

    spread, conv_term = lax.scan(
        backward_offset,
        jnp.zeros((3 * group_count + 1, channels), jnp.float32),
        (ext_index, conv_weight),
    )
    grad_hidden = grad_z + spread[group_count : 2 * group_count]
    for shift_by, margin in (
        (-1, spread[:group_count]),
        (1, spread[2 * group_count : 3 * group_count]),
    ):
        grad_hidden = grad_hidden + passed_along(margin, "vox", shift_by)
    sig = jax.nn.sigmoid(pre)
    grad_pre = (grad_hidden * sig * (1.0 + pre * (1.0 - sig))).astype(jnp.bfloat16)
    grad_rows = to_children(grad_pre, recv_index)
    down_term = contract_first(grouped, grad_rows)
    down_shape = (8, channels, channels)
    up_shape = (channels, 8, channels)
    total_down, total_conv, total_up = lax.psum((down_term, conv_term, up_term), ("vox", "rep"))
    return (
        total_down.astype(jnp.bfloat16).reshape(down_shape),
        total_conv.astype(jnp.bfloat16),
        total_up.astype(jnp.bfloat16).reshape(up_shape),
    )


def solution(mesh):
    return jax.shard_map(
        per_device,
        mesh=mesh,
        in_specs=(
            P("rep", "vox", None),
            P("rep", "vox"),
            P("rep", "vox"),
            P("rep", None, "vox"),
            P("rep", "vox", None),
            P(),
            P(),
            P(),
        ),
        out_specs=(P(), P(), P()),
        check_vma=False,
    )
```

profile of v0, /device:TPU:0, one launch (start us, length us, event | category | flops | bytes accessed | tf_op | source)
XLA Modules:
  0.0 744.5 jit_solution(3736410033572291359)
XLA Ops:
  9.4 7.3 all-to-all-start
  17.4 3.8 broadcast_multiply_fusion.1
  21.2 3.2 copy.36
  24.4 2.8 mul.78
  33.8 3.2 copy.32
  36.9 2.8 mul.72
  50.3 6.0 all-to-all-start.2
  57.6 5.3 all-to-all-done.2
  62.9 3.3 all-to-all-start.1
  67.3 3.8 collective-permute-start
  74.7 6.0 collective-permute-done
  82.0 320.8 %while.23 = (s32[]{:T(128)}, f32[1537,192]{1,0:T(8,128)S(1)}, f32[27,192,192]{2,1,0:T(8,128)}, s32[27,512]{1,0:T(8,128)}, bf16[27,192,192]{2,1,0:T(8,128)(2,1)},...) while((s32[]{:T(128)}, f32[1537,192]{1,0:T(8,128)S(1)}, ...), condition=%wide.region_12.13_spmd, body=%wide.region_10.12_spmd.sunk | while | flops 75598336 | bytes 5356689 | solution.py:135
  89.5 4.3 scatter_fusion
  94.7 2.6 gather_fusion
  101.4 4.3 scatter_fusion
  106.6 2.6 gather_fusion
  113.3 4.3 scatter_fusion
  125.2 4.3 scatter_fusion
  130.3 2.6 gather_fusion
  137.0 4.4 scatter_fusion
  142.2 2.6 gather_fusion
  148.9 4.3 scatter_fusion
  160.8 4.3 scatter_fusion
  166.0 2.6 gather_fusion
  172.7 4.3 scatter_fusion
  184.6 4.3 scatter_fusion
  196.5 4.3 scatter_fusion
  201.6 2.6 gather_fusion
  208.4 4.4 scatter_fusion
  220.3 4.3 scatter_fusion
  225.4 2.6 gather_fusion
  232.1 4.3 scatter_fusion
  237.3 2.6 gather_fusion
  244.0 4.3 scatter_fusion
  255.9 4.3 scatter_fusion
  261.0 2.6 gather_fusion
  267.8 4.3 scatter_fusion
  272.9 2.6 gather_fusion
  279.7 4.3 scatter_fusion
  291.6 4.3 scatter_fusion
  296.7 2.6 gather_fusion
  303.4 4.3 scatter_fusion
  308.6 2.6 gather_fusion
  315.3 4.3 scatter_fusion
  327.2 4.3 scatter_fusion
  339.1 4.3 scatter_fusion
  351.0 4.3 scatter_fusion
  362.8 4.3 scatter_fusion
  374.7 4.3 scatter_fusion
  386.6 4.3 scatter_fusion
  398.5 4.3 scatter_fusion
  405.2 5.9 collective-permute-start.3
  411.1 128.8 %while.24 = (s32[]{:T(128)}, f32[512,192]{0,1:T(8,128)}, s32[27,512]{1,0:T(8,128)}, bf16[1537,192]{1,0:T(8,128)(2,1)S(1)}, bf16[27,192,192]{2,1,0:T(8,128)(2,1)}, /*index=5*/s32[]{:T(128)}, s32[]{:T(128)}) while((s32[]{:T(128)}, f32[512,192]{0,1:T(8,128)}, s32[27,512]{1,0:T(8,128)}, bf16[1537,192]{1,0:T(8,128)(2,1)S(1)}, ...), condition=%wide.region_16.17_spmd.clone, body=%wide.region_15.16_spmd.clone.sunk | while | flops 37947904 | bytes 1487451 | solution.py:116
  543.6 5.5 all-to-all-start.4
  549.4 3.9 copy.40
  553.3 3.8 copy.29
  557.2 4.3 squeeze.36
  561.5 2.6 copy.41
  565.4 2.6 copy.31
  568.0 4.3 squeeze.31
  579.9 6.0 all-to-all-start.3
  585.9 3.8 fusion.7
  595.1 3.3 fusion.9
  598.4 143.5 %all-reduce.6 = (bf16[1536,192]{0,1:T(8,128)(2,1)S(1)}, bf16[27,192,192]{2,1,0:T(8,128)(2,1)}, bf16[192,1536]{1,0:T(8,128)(2,1)S(1)}) all-reduce(f32[1536,192]{0,1:T(8,128)} %fusion.9, f32[27,192,192]{2,1,0:T(8,128)} %get-tuple-element.69, f32[192,1536]{1,0:T(8,128)S(1)} %copy-done.7), channel_id=1, replica_groups=mesh['vox'=8,'rep'=4] {'vox','rep'}, use_global_device_ids=true, to_apply=%region_13.14 | all-reduce | flops 1585152 | bytes 9510912 | tf_op jit(solution)/shard_map/psum | solution.py:152
  (467 shorter events, 356.8 us)
Async XLA Ops:
  0.6 26.5 %copy-start = (bf16[8,192,192]{2,1,0:T(8,128)(2,1)S(1)}, bf16[8,192,192]{2,1,0:T(8,128)(2,1)}, u32[]{:S(2)}) copy-start(bf16[8,192,192]{2,1,0:T(8,128)(2,1)} %param.17) | copy-start | bytes 1769476
  3.4 17.8 %copy-start.12 = (pred[512]{0:T(512)(128)(4,1)}, pred[512]{0:T(512)(128)(4,1)S(1)}, u32[]{:S(2)}) copy-start(pred[512]{0:T(512)(128)(4,1)S(1)} %get-tuple-element.130) | copy-start | bytes 1540
  9.4 40.9 %all-to-all-start = ((s32[8,1,2]{2,1,0:T(1,128)}), s32[8,1,2]{2,1,0:T(1,128)S(1)}, u32[]{:S(2)}, u32[]{:S(2)}) async-start(s32[8,1,2]{2,1,0:T(1,128)} %bitcast.14), calls=%async_computation | async-start | bytes 8192 | tf_op jit(solution)/shard_map/all_to_all | solution.py:75
  41.5 7.5 %copy-start.10 = (s32[1,27,512]{2,0,1:T(1,128)S(1)}, s32[1,27,512]{2,0,1:T(1,128)}, u32[]{:S(2)}) copy-start(s32[1,27,512]{2,0,1:T(1,128)} %param.15) | copy-start | bytes 165892
  50.3 12.6 %all-to-all-start.2 = ((f32[8,2,192]{2,1,0:T(2,128)}), f32[8,2,192]{2,1,0:T(2,128)S(1)}, u32[]{:S(2)}, u32[]{:S(2)}) async-start(f32[8,2,192]{2,1,0:T(2,128)} %reshape.420), calls=%async_computation.2 | async-start | bytes 32768 | tf_op jit(solution)/shard_map/all_to_all | solution.py:68
  62.9 10.8 %all-to-all-start.1 = ((f32[8,2,192]{2,1,0:T(2,128)}), f32[8,2,192]{2,1,0:T(2,128)S(1)}, u32[]{:S(2)}, u32[]{:S(2)}) async-start(f32[8,2,192]{2,1,0:T(2,128)} %reshape.417), calls=%async_computation.1 | async-start | bytes 32768 | tf_op jit(solution)/shard_map/all_to_all | solution.py:68
  67.2 13.5 %copy-start.3 = (f32[512,192]{1,0:T(8,128)}, f32[512,192]{1,0:T(8,128)S(1)}, u32[]{:S(2)}) copy-start(f32[512,192]{1,0:T(8,128)S(1)} %scatter_fusion.2) | copy-start | bytes 1179652
  67.3 13.3 %collective-permute-start = (bf16[512,192]{1,0:T(8,128)(2,1)S(1)}, bf16[512,192]{1,0:T(8,128)(2,1)S(1)}, u32[]{:S(2)}, u32[]{:S(2)}) collective-permute-start(bf16[512,192]{1,0:T(8,128)(2,1)S(1)} %multiply_convert_fusion.1), channel_id=1, source_target_pairs={{0,4},{4,8},{8,12},{12,16},{16,20},{20,24},{24,28},{1,5},{5,9},{9,... | collective-permute-start | bytes 589832 | tf_op jit(solution)/shard_map/ppermute | solution.py:16
  71.2 9.5 %collective-permute-start.1 = (bf16[512,192]{1,0:T(8,128)(2,1)S(1)}, bf16[512,192]{1,0:T(8,128)(2,1)}, u32[]{:S(2)}, u32[]{:S(2)}) collective-permute-start(bf16[512,192]{1,0:T(8,128)(2,1)S(1)} %multiply_convert_fusion.1), channel_id=1, source_target_pairs={{4,0},{8,4},{12,8},{16,12},{20,16},{24,20},{28,24},{5,1},{9,5},{13... | collective-permute-start | bytes 589832 | tf_op jit(solution)/shard_map/ppermute | solution.py:17
  74.6 6.1 copy-start.6
  82.0 5.3 copy-start.1
  89.5 4.4 copy-start.2
  93.9 5.3 copy-start.1
  101.4 4.4 copy-start.2
  105.8 5.3 copy-start.1
  113.3 4.3 copy-start.2
  117.7 5.3 copy-start.1
  125.2 4.4 copy-start.2
  129.5 5.2 copy-start.1
  137.0 4.4 copy-start.2
  141.4 5.3 copy-start.1
  148.9 4.4 copy-start.2
  153.3 5.3 copy-start.1
  160.8 4.3 copy-start.2
  165.2 5.3 copy-start.1
  172.7 4.4 copy-start.2
  177.1 5.3 copy-start.1
  184.6 4.3 copy-start.2
  189.0 5.3 copy-start.1
  196.5 4.3 copy-start.2
  200.8 5.3 copy-start.1
  208.3 4.4 copy-start.2
  212.8 5.3 copy-start.1
  220.3 4.3 copy-start.2
  224.6 5.2 copy-start.1
  232.1 4.3 copy-start.2
  236.5 5.2 copy-start.1
  244.0 4.3 copy-start.2
  248.4 5.2 copy-start.1
  255.9 4.4 copy-start.2
  260.2 5.3 copy-start.1
  267.8 4.3 copy-start.2
  272.1 5.3 copy-start.1
  279.7 4.3 copy-start.2
  284.0 5.3 copy-start.1
  295.9 5.3 copy-start.1
  307.8 5.3 copy-start.1
  315.3 4.4 copy-start.2
  319.7 5.3 copy-start.1
  331.6 5.2 copy-start.1
  343.4 5.3 copy-start.1
  355.3 5.3 copy-start.1
  362.8 4.4 copy-start.2
  367.2 5.3 copy-start.1
  379.1 5.3 copy-start.1
  391.0 5.3 copy-start.1
  398.5 4.4 copy-start.2
  403.9 173.0 %collective-permute-start.2 = (f32[512,192]{1,0:T(8,128)}, f32[512,192]{1,0:T(8,128)}, u32[]{:S(2)}, u32[]{:S(2)}) collective-permute-start(f32[512,192]{1,0:T(8,128)} %get-tuple-element.134), channel_id=1, source_target_pairs={{4,0},{8,4},{12,8},{16,12},{20,16},{24,20},{28,24},{5,1},{9,5},{13... | collective-permute-start | bytes 1179656 | tf_op jit(solution)/shard_map/ppermute | solution.py:25
  405.2 171.7 %collective-permute-start.3 = (f32[512,192]{1,0:T(8,128)}, f32[512,192]{1,0:T(8,128)}, u32[]{:S(2)}, u32[]{:S(2)}) collective-permute-start(f32[512,192]{1,0:T(8,128)} %get-tuple-element.135), channel_id=1, source_target_pairs={{0,4},{4,8},{8,12},{12,16},{16,20},{20,24},{24,28},{1,5},{5,9},{9,... | collective-permute-start | bytes 1179656 | tf_op jit(solution)/shard_map/ppermute | solution.py:25
  539.8 9.4 %copy-start.14 = (s32[512,1]{0,1:T(1,128)S(1)}, s32[512,1]{0,1:T(1,128)}, u32[]{:S(2)}) copy-start(s32[512,1]{0,1:T(1,128)} %get-tuple-element.125) | copy-start | bytes 6148
  539.8 9.4 %copy-start.9 = (bf16[4096]{0:T(1024)(128)(2,1)S(1)}, bf16[4096]{0:T(1024)(128)(2,1)}, u32[]{:S(2)}) copy-start(bf16[4096]{0:T(1024)(128)(2,1)} %copy-done.8) | copy-start | bytes 24580
  543.6 30.7 %all-to-all-start.4 = ((bf16[8,2,192]{2,1,0:T(2,128)(2,1)}), bf16[8,2,192]{2,1,0:T(2,128)(2,1)S(1)}, u32[]{:S(2)}, u32[]{:S(2)}) async-start(bf16[8,2,192]{2,1,0:T(2,128)(2,1)} %reshape.425), calls=%async_computation.4 | async-start | bytes 16384 | tf_op jit(solution)/shard_map/all_to_all | solution.py:90
  576.9 9.0 %copy-start.13 = (pred[512]{0:T(512)(128)(4,1)S(1)}, pred[512]{0:T(512)(128)(4,1)}, u32[]{:S(2)}) copy-start(pred[512]{0:T(512)(128)(4,1)} %copy-done.12) | copy-start | bytes 1540
  579.9 12.5 %all-to-all-start.3 = ((bf16[8,2,192]{2,1,0:T(2,128)(2,1)}), bf16[8,2,192]{2,1,0:T(2,128)(2,1)S(1)}, u32[]{:S(2)}, u32[]{:S(2)}) async-start(bf16[8,2,192]{2,1,0:T(2,128)(2,1)} %reshape.422), calls=%async_computation.3 | async-start | bytes 16384 | tf_op jit(solution)/shard_map/all_to_all | solution.py:90
  (12 other events, 45.0 us)
where the time goes:
time: 752 us; the launch traced here: 744 us
  local copies, waits for them, and re-layouts  218 us (29%)
  other arithmetic  177 us (24%)
  matrix products  151 us (20%)
  blocking collectives  143 us (19%)
  starting transfers between devices  40.4 us (5%)
  waiting for transfers between devices  11.5 us (2%)
    psum x1, blocking collectives, per_device(): lax.psum((down_term, conv_term, up_term), ('vox', 'rep'))  143 us
    scatter-add x27, other arithmetic, backward_offset(): spread_now.at[index_row].add(contract_last(dz_half, weight_here))  117 us
    gather x27, local copies, waits for them, and re-layouts, backward_offset(): rows_here = extended[index_row]  69.6 us
    dot_general x29, matrix products, contract_first(): lax.dot_general(left, right, (((0,), (0,)), ((), ())), preferred_element_...  57.8 us
    dot_general x27, matrix products, forward_offset(): jnp.dot(rows_here, weight_here, preferred_element_type=jnp.float32)  55.9 us
    gather x27, local copies, waits for them, and re-layouts, forward_offset(): rows_here = extended[index_row]  52.7 us
    dot_general x28, matrix products, contract_last(): lax.dot_general(left, right, (((1,), (1,)), ((), ())), preferred_element_...  35.7 us
    dot_general x27, local copies, waits for them, and re-layouts, contract_last(): lax.dot_general(left, right, (((1,), (1,)), ((), ())), preferred_element_...  26.9 us
  transfers between devices with their start and end apart: 9, of which 3 were waited for; matrix products, arithmetic and copies ran while one was open for 27% of the time, Pallas kernels for 0%

commit v1 on v0

v1 whole, which is shorter than its diff:
```python
import jax
import jax.numpy as jnp
from jax import lax
from jax.experimental import pallas as pl
from jax.experimental.pallas import tpu as pltpu
from jax.sharding import PartitionSpec as P

CAP = 2


def dot(left, right, dims, precision=None):
    return lax.dot_general(
        left, right, (dims, ((), ())), precision=precision, preferred_element_type=jnp.float32
    )


def conv_kernel(
    before, own, after, wide, ids_out, ids_in, weight, term_ref, both_ref, acc_up, acc_down
):
    step = pl.program_id(0)
    channels, count = acc_up.shape

    @pl.when(step == 0)
    def _():
        acc_up[...] = jnp.zeros_like(acc_up)
        acc_down[...] = jnp.zeros_like(acc_down)

    rows = lax.broadcasted_iota(jnp.int32, (count, count), 0)

    def hot(ids):
        return jnp.where(rows == ids, 1.0, 0.0).astype(jnp.bfloat16)

    weight_here = weight[0]
    gathered = jnp.zeros((channels, count), jnp.float32)
    spread = acc_down[...]
    for at, block in enumerate((before, own, after)):
        gathered += dot(
            block[:channels, :], hot(ids_out[0] - at * count), ((1,), (0,))
        )
        moved = dot(weight_here, block[channels:, :], ((1,), (0,))).astype(jnp.bfloat16)
        spread += dot(moved, hot(ids_in[0, :, at * count : (at + 1) * count]), ((1,), (1,)))
    acc_down[...] = spread
    gathered = gathered.astype(jnp.bfloat16)
    acc_up[...] += dot(weight_here, gathered, ((0,), (0,)))
    term_ref[0] = dot(gathered, own[channels:, :], ((1,), (1,)))

    @pl.when(step == pl.num_programs(0) - 1)
    def _():
        upper = own[:channels, :].astype(jnp.float32) + acc_up[...]
        both_ref[:channels, :] = upper.astype(jnp.bfloat16)
        pre = wide[:channels, :]
        sig = jax.nn.sigmoid(pre)
        slope = sig * (1.0 + pre * (1.0 - sig))
        both_ref[channels:, :] = ((wide[channels:, :] + acc_down[...]) * slope).astype(
            jnp.bfloat16
        )


def conv_call(before, own, after, wide, ids_out, ids_in, conv_weight):
    offsets, channels = conv_weight.shape[:2]
    count = own.shape[1]
    whole = lambda j: (0, 0)
    each = lambda j: (j, 0, 0)
    return pl.pallas_call(
        conv_kernel,
        grid=(offsets,),
        in_specs=[pl.BlockSpec((2 * channels, count), whole)] * 4
        + [
            pl.BlockSpec((1, 1, count), each),
            pl.BlockSpec((1, 1, 3 * count), each),
            pl.BlockSpec((1, channels, channels), each),
        ],
        out_specs=[
            pl.BlockSpec((1, channels, channels), each),
            pl.BlockSpec((2 * channels, count), whole),
        ],
        out_shape=[
            jax.ShapeDtypeStruct((offsets, channels, channels), jnp.float32),
            jax.ShapeDtypeStruct((2 * channels, count), jnp.bfloat16),
        ],
        scratch_shapes=[pltpu.VMEM((channels, count), jnp.float32)] * 2,
        compiler_params=pltpu.CompilerParams(vmem_limit_bytes=48 * 1024 * 1024),
    )(before, own, after, wide, ids_out, ids_in, conv_weight)


def per_device(
    fine_feats, occupancy, parent, neighbors, cotangent, down_weight, conv_weight, up_weight
):
    fine_rows = fine_feats[0]
    occupied = occupancy[0]
    parents = parent[0]
    near_ids = neighbors[0]
    cot_rows = cotangent[0]
    channels = fine_rows.shape[1]
    count = parents.shape[0]
    vox_count = lax.axis_size("vox")
    slots = vox_count * CAP
    own_index = lax.axis_index("vox")
    up = [(i, i + 1) for i in range(vox_count - 1)]
    down = [(j, i) for i, j in up]
    exact = lax.Precision.HIGHEST

    near_next = near_ids + 1
    lists = jnp.concatenate(
        [lax.ppermute(near_next, "vox", up), near_next, lax.ppermute(near_next, "vox", down)], 1
    )
    ids_in = (lists - 1 - own_index * count)[:, None, :]
    ids_out = jnp.where(near_ids < 0, -1, near_ids - (own_index - 1) * count)[:, None, :]

    owner = parents // count
    local_id = parents % count
    remote = owner != own_index
    owner_hits = (
        (owner[:, None] == jnp.arange(vox_count, dtype=jnp.int32)[None, :]) & remote[:, None]
    ).astype(jnp.int32)
    ranks = jnp.cumsum(owner_hits, axis=0) - 1
    slot = jnp.sum(ranks * owner_hits, axis=1)
    dest = jnp.where(remote, owner * CAP + slot, slots)
    place = jnp.arange(slots, dtype=jnp.int32)[:, None] == dest[None, :]
    send_ids = jnp.sum(jnp.where(place, local_id[None, :] + 1, 0), axis=1)

    mask_half = occupied.astype(jnp.bfloat16)[:, None]
    grouped = (fine_rows * mask_half).reshape(count, 8 * channels)
    cot_groups = (cot_rows * mask_half).reshape(count, 8 * channels)
    pre_groups = dot(grouped, down_weight.reshape(8 * channels, channels), ((1,), (0,)))
    back_groups = dot(cot_groups, up_weight.reshape(channels, 8 * channels), ((1,), (1,)))
    values = jnp.concatenate([pre_groups, back_groups], 1)
    send = dot(place.astype(jnp.float32), values, ((1,), (0,)), exact)
    tail = jnp.broadcast_to(send_ids.astype(jnp.float32)[:, None], (slots, 128))
    send = jnp.concatenate([send, tail], 1).reshape(vox_count, CAP, 2 * channels + 128)
    got = lax.all_to_all(send, "vox", split_axis=0, concat_axis=0, tiled=True)
    got = got.reshape(slots, 2 * channels + 128)
    recv_index = got[:, 2 * channels].astype(jnp.int32) - 1
    coarse_ids = jnp.arange(count, dtype=jnp.int32)[:, None]
    keep = coarse_ids == jnp.where(remote, -1, local_id)[None, :]
    arrived = coarse_ids == recv_index[None, :]
    wide = dot(values, keep.astype(jnp.float32), ((0,), (1,)), exact) + dot(
        got[:, : 2 * channels], arrived.astype(jnp.float32), ((0,), (1,)), exact
    )
    own = jnp.concatenate([jax.nn.silu(wide[:channels]), wide[channels:]], 0).astype(jnp.bfloat16)
    before = lax.ppermute(own, "vox", up)
    after = lax.ppermute(own, "vox", down)
    conv_term, both = conv_call(before, own, after, wide, ids_out, ids_in, conv_weight)

    outgoing = dot(arrived.astype(jnp.bfloat16), both, ((0,), (1,))).astype(jnp.bfloat16)
    returned = lax.all_to_all(
        outgoing.reshape(vox_count, CAP, 2 * channels),
        "vox",
        split_axis=0,
        concat_axis=0,
        tiled=True,
    ).reshape(slots, 2 * channels)
    rows = dot(both, keep.astype(jnp.bfloat16), ((1,), (0,))) + dot(
        returned, place.astype(jnp.bfloat16), ((0,), (0,))
    )
    rows = rows.astype(jnp.bfloat16)
    up_term = dot(rows[:channels], cot_groups, ((1,), (0,)))
    down_term = dot(grouped, rows[channels:], ((0,), (1,)))
    total_down, total_conv, total_up = lax.psum((down_term, conv_term, up_term), ("vox", "rep"))
    return (
        total_down.astype(jnp.bfloat16).reshape(8, channels, channels),
        total_conv.astype(jnp.bfloat16),
        total_up.astype(jnp.bfloat16).reshape(channels, 8, channels),
    )


def solution(mesh):
    return jax.shard_map(
        per_device,
        mesh=mesh,
        in_specs=(
            P("rep", "vox", None),
            P("rep", "vox"),
            P("rep", "vox"),
            P("rep", None, "vox"),
            P("rep", "vox", None),
            P(),
            P(),
            P(),
        ),
        out_specs=(P(), P(), P()),
        check_vma=False,
    )
```

time: 752 us -> 285 us (0.38)
  local copies, waits for them, and re-layouts: 218 us -> 43.4 us
  other arithmetic: 177 us -> 10.6 us
  matrix products: 151 us -> 7.92 us
  Pallas kernels: 0 us -> 38.8 us
  starting transfers between devices: 40.4 us -> 21.5 us
    dot_general x85 -> x10, matrix products: 151 us -> 7.92 us  [dot(): lax.dot_general(left, right, (dims, ((), ())), precision=precision, prefe...]
    gather x60 -> x0, local copies, waits for them, and re-layouts: 133 us -> none  [the longest x27 69.6 us: backward_offset(): rows_here = extended[index_row]]
    scatter-add x29 -> x0, other arithmetic: 119 us -> none  [the longest x27 117 us: backward_offset(): spread_now.at[index_row].add(contract_last(dz_half, weight_here))]
    select_n x60 -> x2, other arithmetic: 44 us -> 0.76 us  [the longest x1 0.7 us: per_device(): dest = jnp.where(remote, owner * CAP + slot, slots)]
    pallas_call x0 -> x1, Pallas kernels: none -> 38.8 us  [conv_call(): pl.pallas_call(conv_kernel, grid=(offsets,), in_specs=[pl.BlockSpec((2 *...]
    dot_general x27 -> x0, local copies, waits for them, and re-layouts: 26.9 us -> none  [contract_last(): lax.dot_general(left, right, (((1,), (1,)), ((), ())), preferred_element_...]
    all_to_all x5 -> x2, starting transfers between devices: 28.1 us -> 10.5 us  [the longest x1 5.61 us: per_device(): got = lax.all_to_all(send, 'vox', split_axis=0, concat_axis=0, tiled=True)]
    scatter x5 -> x0, local copies, waits for them, and re-layouts: 11.8 us -> none  [the longest x2 4.75 us: to_coarse(): jnp.zeros((group_count, channels), jnp.float32).at[keep_local]]
  transfers between devices with their start and end apart: 9 -> 6, of which waited for: 3 -> 2; matrix products, arithmetic and copies ran while one was open for 27% -> 17% of each run, Pallas kernels for 0% -> 0%
where the time goes in v1:
time: 285 us; the launch traced here: 284 us
  blocking collectives  144 us (51%)
  local copies, waits for them, and re-layouts  43.4 us (15%)
  Pallas kernels  38.8 us (14%)
  starting transfers between devices  21.5 us (8%)
  waiting for transfers between devices  17.2 us (6%)
  other arithmetic  10.6 us (4%)
  matrix products  7.92 us (3%)
    psum x1, blocking collectives, per_device(): lax.psum((down_term, conv_term, up_term), ('vox', 'rep'))  144 us
    pallas_call x1, Pallas kernels, conv_call(): pl.pallas_call(conv_kernel, grid=(offsets,), in_specs=[pl.BlockSpec((2 *...  38.8 us
    unnamed x23, local copies, waits for them, and re-layouts  13 us
    ppermute x1, waiting for transfers between devices, per_device(): before = lax.ppermute(own, 'vox', up)  11.4 us
    dot_general x10, matrix products, dot(): lax.dot_general(left, right, (dims, ((), ())), precision=precision, prefe...  7.92 us
    mul x4, local copies, waits for them, and re-layouts, per_device(): grouped = (fine_rows * mask_half).reshape(count, 8 * channels)  7.66 us
    ppermute x1, starting transfers between devices, per_device(): lax.ppermute(near_next, 'vox', up)  6.1 us
    mul x2, local copies, waits for them, and re-layouts, per_device(): cot_groups = (cot_rows * mask_half).reshape(count, 8 * channels)  5.93 us
  transfers between devices with their start and end apart: 6, of which 2 were waited for; matrix products, arithmetic and copies ran while one was open for 17% of the time, Pallas kernels for 0%

profile of v1, /device:TPU:0, one launch (start us, length us, event | category | flops | bytes accessed | tf_op | source)
XLA Modules:
  0.0 284.3 jit_solution(1287510961615806007)
XLA Ops:
  0.6 0.0 copy-start
  0.6 1.5 fusion.16
  2.2 1.3 collective-permute-start.3
  3.5 6.1 %collective-permute-start.2 = (s32[27,512]{1,0:T(8,128)}, s32[27,512]{1,0:T(8,128)}, u32[]{:S(2)}, u32[]{:S(2)}) collective-permute-start(s32[27,512]{1,0:T(8,128)} %get-tuple-element.30), channel_id=1, source_target_pairs={{0,4},{4,8},{8,12},{12,16},{16,20},{20,24},{24,28},{1,5},{5,9},{9,... | collective-permute-start | bytes 165896 | tf_op jit(solution)/shard_map/ppermute | solution.py:105
  9.6 0.7 broadcast_compare_fusion
  10.3 1.1 reduce-window.6
  11.4 0.2 slice_reduce_fusion
  11.7 0.7 broadcast_compare_fusion.1
  12.4 0.1 fusion.21
  12.5 0.7 compare_select_fusion.4
  13.2 0.1 select_reduce_fusion
  13.3 0.5 convert_element_type.60
  13.8 0.8 convert_reduce_fusion
  14.6 3.8 %broadcast_multiply_fusion.1 = (bf16[1,4096,192]{1,2,0:T(8,128)(2,1)}, bf16[1,4096,192]{1,2,0:T(8,128)(2,1)}) fusion(bf16[1,4096,192]{1,2,0:T(8,128)(2,1)} %param.8, bf16[4096]{0:T(1024)(128)(2,1)S(1)} %convert_reduce_fusion, bf16[1,4096,192]{1,2,0:T(8,128)(2,1)} %param.12), kind=kLoop, calls=%fused_computation.12 | loop fusion | flops 1572864 | bytes 6299648 | tf_op jit(solution)/shard_map/mul | solution.py:123
  18.4 3.1 %copy.42 = bf16[1,4096,192]{2,1,0:T(8,128)(2,1)S(1)} copy(bf16[1,4096,192]{1,2,0:T(8,128)(2,1)} %get-tuple-element.32) | data formatting | bytes 3145728 | tf_op jit(solution)/shard_map/mul | solution.py:124
  21.5 2.8 mul.57
  24.3 1.8 reshape.216
  26.1 3.2 %copy.41 = bf16[1,4096,192]{2,1,0:T(8,128)(2,1)S(1)} copy(bf16[1,4096,192]{1,2,0:T(8,128)(2,1)} %get-tuple-element.31) | data formatting | bytes 3145728 | tf_op jit(solution)/shard_map/mul | solution.py:123
  29.3 2.8 mul.55
  32.0 2.2 fusion.36
  34.3 0.0 copy-start.9
  34.3 0.7 fusion.35
  35.0 0.5 fusion.6
  35.4 0.1 broadcast_in_dim.46
  35.5 0.6 reshape.218
  36.1 5.6 %all-to-all-start = ((f32[8,2,512]{2,1,0:T(2,128)}), f32[8,2,512]{2,1,0:T(2,128)S(1)}, u32[]{:S(2)}, u32[]{:S(2)}) async-start(f32[8,2,512]{2,1,0:T(2,128)} %reshape.218), calls=%async_computation | async-start | bytes 65536 | tf_op jit(solution)/shard_map/all_to_all | solution.py:131
  41.8 0.9 fusion.5
  42.6 5.8 %all-to-all-done = f32[8,2,512]{2,1,0:T(2,128)S(1)} async-done(((f32[8,2,512]{2,1,0:T(2,128)}), f32[8,2,512]{2,1,0:T(2,128)S(1)}, u32[]{:S(2)}, u32[]{:S(2)}) %all-to-all-start) | async-done | bytes 32800 | tf_op jit(solution)/shard_map/all_to_all | solution.py:131
  48.5 0.1 fusion.28
  48.6 0.5 convolution_add_fusion.1.wide
  49.1 0.1 multiply_convert_fusion
  49.3 2.4 collective-permute-start
  51.7 1.3 collective-permute-start.1
  53.0 0.1 fusion.18.ids_out
  53.1 0.1 copy.45
  53.2 0.0 collective-permute-done.2
  53.2 0.9 copy.44
  54.1 0.9 concatenate.31
  55.0 0.2 fusion.12.ids_in
  55.1 11.4 %collective-permute-done.before = bf16[384,512]{1,0:T(8,128)(2,1)S(1)} collective-permute-done((bf16[384,512]{1,0:T(8,128)(2,1)S(1)}, bf16[384,512]{1,0:T(8,128)(2,1)S(1)}, u32[]{:S(2)}, u32[]{:S(2)}) %collective-permute-start) | collective-permute-done | bytes 393248 | tf_op jit(solution)/shard_map/ppermute | solution.py:141
  66.5 1.7 copy-done.1
  68.3 38.8 %shard_map.103 = (f32[27,192,192]{2,1,0:T(8,128)}, bf16[384,512]{1,0:T(8,128)(2,1)S(1)}) custom-call(bf16[384,512]{1,0:T(8,128)(2,1)S(1)} %collective-permute-done.before, bf16[384,512]{1,0:T(8,128)(2,1)S(1)} %pad_maximum_fusion.3.own, bf16[384,512]{1,0:T(8,128)(2,1)S(1)} %collective-permute-done.1.after, f32[384,512]{1,0:T(8,128)S(1)} %convolution_add_fusion.1.wide, ...), custom_call_target="tpu_custom_call" | custom-call | tf_op jit(solution)/shard_map/pallas_call | solution.py:64
  107.0 0.2 convolution_convert_fusion
  107.3 0.6 reshape.220
  107.9 4.8 %all-to-all-start.1 = ((bf16[8,2,384]{2,1,0:T(2,128)(2,1)}), bf16[8,2,384]{2,1,0:T(2,128)(2,1)S(1)}, u32[]{:S(2)}, u32[]{:S(2)}) async-start(bf16[8,2,384]{2,1,0:T(2,128)(2,1)} %reshape.220), calls=%async_computation.1 | async-start | bytes 24576 | tf_op jit(solution)/shard_map/all_to_all | solution.py:146
  112.8 0.2 convert_element_type.57
  112.9 3.2 %copy.46 = bf16[1,4096,192]{2,1,0:T(8,128)(2,1)S(1)} copy(bf16[1,4096,192]{1,2,0:T(8,128)(2,1)} %param.12) | data formatting | bytes 3145728 | tf_op args[4]
  116.1 3.8 %copy.38 = bf16[1,4096,192]{2,1,0:T(8,128)(2,1)} copy(bf16[1,4096,192]{1,2,0:T(8,128)(2,1)} %param.8) | data formatting | bytes 3145728 | tf_op args[0]
  119.9 0.1 copy.39
  120.0 2.8 squeeze.17
  122.8 2.6 copy.47
  125.4 0.1 mul.50
  125.6 1.6 copy.40
  127.2 4.3 %squeeze.14 = bf16[512,1536]{1,0:T(8,128)(2,1)} reshape(bf16[1,4096,192]{2,1,0:T(8,128)(2,1)} %copy.38) | data formatting | bytes 3145728 | tf_op jit(solution)/shard_map/squeeze | solution.py:89
  131.5 0.3 fusion.19
  131.8 0.4 fusion.4
  132.3 0.7 copy-done.2
  132.9 1.7 fusion
  134.6 0.6 copy-done.4
  135.2 0.5 fusion.2
  135.8 0.7 copy-done.6
  136.5 144.0 %all-reduce.2 = (bf16[1536,192]{0,1:T(8,128)(2,1)}, bf16[27,192,192]{2,1,0:T(8,128)(2,1)}, bf16[192,1536]{1,0:T(8,128)(2,1)}) all-reduce(f32[1536,192]{0,1:T(8,128)S(1)} %fusion.2, f32[27,192,192]{2,1,0:T(8,128)} %get-tuple-element.6, f32[192,1536]{1,0:T(8,128)S(1)} %copy-done.6), channel_id=1, replica_groups=mesh['vox'=8,'rep'=4] {'vox','rep'}, use_global_device_ids=true, to_apply=%region_4.5 | all-reduce | flops 1585152 | bytes 9510912 | tf_op jit(solution)/shard_map/psum | solution.py:159
  280.5 2.3 copy.49
  282.8 1.5 reshape.223
  (26 shorter events, 0.2 us)
Async XLA Ops:
  0.6 33.6 %copy-start = (bf16[8,192,192]{2,1,0:T(8,128)(2,1)S(1)}, bf16[8,192,192]{2,1,0:T(8,128)(2,1)}, u32[]{:S(2)}) copy-start(bf16[8,192,192]{2,1,0:T(8,128)(2,1)} %param.13) | copy-start | bytes 1769476
  2.2 51.9 %collective-permute-start.3 = (s32[27,512]{1,0:T(8,128)}, s32[27,512]{1,0:T(8,128)}, u32[]{:S(2)}, u32[]{:S(2)}) collective-permute-start(s32[27,512]{1,0:T(8,128)} %get-tuple-element.30), channel_id=1, source_target_pairs={{4,0},{8,4},{12,8},{16,12},{20,16},{24,20},{28,24},{5,1},{9,5},{13... | collective-permute-start | bytes 165896 | tf_op jit(solution)/shard_map/ppermute | solution.py:105
  3.5 49.7 %collective-permute-start.2 = (s32[27,512]{1,0:T(8,128)}, s32[27,512]{1,0:T(8,128)}, u32[]{:S(2)}, u32[]{:S(2)}) collective-permute-start(s32[27,512]{1,0:T(8,128)} %get-tuple-element.30), channel_id=1, source_target_pairs={{0,4},{4,8},{8,12},{12,16},{16,20},{20,24},{24,28},{1,5},{5,9},{9,... | collective-permute-start | bytes 165896 | tf_op jit(solution)/shard_map/ppermute | solution.py:105
  32.0 2.2 copy-start.5
  34.3 1.2 copy-start.9
  36.1 12.3 %all-to-all-start = ((f32[8,2,512]{2,1,0:T(2,128)}), f32[8,2,512]{2,1,0:T(2,128)S(1)}, u32[]{:S(2)}, u32[]{:S(2)}) async-start(f32[8,2,512]{2,1,0:T(2,128)} %reshape.218), calls=%async_computation | async-start | bytes 65536 | tf_op jit(solution)/shard_map/all_to_all | solution.py:131
  48.6 4.4 %copy-start.8 = (s32[1,27,512]{2,0,1:T(1,128)S(1)}, s32[1,27,512]{2,0,1:T(1,128)}, u32[]{:S(2)}) copy-start(s32[1,27,512]{2,0,1:T(1,128)} %param.11) | copy-start | bytes 165892
  49.3 17.2 %collective-permute-start = (bf16[384,512]{1,0:T(8,128)(2,1)S(1)}, bf16[384,512]{1,0:T(8,128)(2,1)S(1)}, u32[]{:S(2)}, u32[]{:S(2)}) collective-permute-start(bf16[384,512]{1,0:T(8,128)(2,1)S(1)} %pad_maximum_fusion.3.own), channel_id=1, source_target_pairs={{0,4},{4,8},{8,12},{12,16},{16,20},{20,24},{24,28},{1,5},{5,9},{9,... | collective-permute-start | bytes 1179656 | tf_op jit(solution)/shard_map/ppermute | solution.py:141
  51.7 14.8 %collective-permute-start.1 = (bf16[384,512]{1,0:T(8,128)(2,1)S(1)}, bf16[384,512]{1,0:T(8,128)(2,1)S(1)}, u32[]{:S(2)}, u32[]{:S(2)}) collective-permute-start(bf16[384,512]{1,0:T(8,128)(2,1)S(1)} %pad_maximum_fusion.3.own), channel_id=1, source_target_pairs={{4,0},{8,4},{12,8},{16,12},{20,16},{24,20},{28,24},{5,1},{9,5},{13... | collective-permute-start | bytes 1179656 | tf_op jit(solution)/shard_map/ppermute | solution.py:142
  66.5 1.8 copy-start.1
  107.9 23.6 %all-to-all-start.1 = ((bf16[8,2,384]{2,1,0:T(2,128)(2,1)}), bf16[8,2,384]{2,1,0:T(2,128)(2,1)S(1)}, u32[]{:S(2)}, u32[]{:S(2)}) async-start(bf16[8,2,384]{2,1,0:T(2,128)(2,1)} %reshape.220), calls=%async_computation.1 | async-start | bytes 24576 | tf_op jit(solution)/shard_map/all_to_all | solution.py:146
  131.5 1.4 copy-start.2
  132.9 1.7 copy-start.3
  132.9 2.3 copy-start.4
  135.2 1.3 copy-start.6
  280.5 2.3 copy-start.7

commit v2 on v1

--- a/solution.py
+++ b/solution.py
@@ -83,6 +83,218 @@
     )(before, own, after, wide, ids_out, ids_in, conv_weight)
 
 
+UNIT = 16
+PIECES = (5 * UNIT, 4 * UNIT)
+FAR = 4
+
+
+def reduce_kernel(x_ref, out_ref, acc, got_core, got_one, got_two, got_far, send, recv):
+    v, r = lax.axis_index("vox"), lax.axis_index("rep")
+    z, x = v // 2, v % 2
+    y, core = r // 2, r % 2
+    core_peer = (v, y * 2 + (1 - core))
+    y_peer = (v, (1 - y) * 2 + core)
+    x_peer = (z * 2 + (1 - x), r)
+    far_peers = [(((z + k) % FAR) * 2 + x, r) for k in range(1, FAR)]
+    mesh_ids = pl.DeviceIdType.MESH
+
+    barrier = pltpu.get_barrier_semaphore()
+    peers = [core_peer, y_peer, x_peer] + far_peers
+    for peer in peers:
+        pl.semaphore_signal(barrier, inc=1, device_id=peer, device_id_type=mesh_ids)
+    pl.semaphore_wait(barrier, len(peers))
+
+    used = [0]
+
+    def push(source, target, peer):
+        at = used[0]
+        used[0] += 1
+        copy = pltpu.make_async_remote_copy(
+            src_ref=source,
+            dst_ref=target,
+            send_sem=send.at[at],
+            recv_sem=recv.at[at],
+            device_id=peer,
+            device_id_type=mesh_ids,
+        )
+        copy.start()
+        return copy
+
+    def at(start, size):
+        return pl.ds(pl.multiple_of(start, UNIT), size)
+
+    def add(target, target_at, left, left_at, others, size):
+        def body(i, carry):
+            step = i * UNIT
+            total = left[at(left_at + step, UNIT), :].astype(jnp.float32)
+            for ref, ref_at in others:
+                total += ref[at(ref_at + step, UNIT), :].astype(jnp.float32)
+            target[at(target_at + step, UNIT), :] = total.astype(target.dtype)
+            return carry
+
+        lax.fori_loop(0, size // UNIT, body, 0)
+
+    half = 4 * FAR * sum(PIECES)
+    base = [0, 4 * FAR * PIECES[0]]
+    whole = [4 * FAR * p for p in PIECES]
+    first_peer, second_peer = (y_peer, x_peer), (x_peer, y_peer)
+    first_bit, second_bit = (y, x), (x, y)
+    mine, other = core * half, (1 - core) * half
+    sent = []
+
+    core_copies = [
+        push(x_ref.at[at(other + base[s], whole[s])], got_core.at[at(base[s], whole[s])], core_peer)
+        for s in (0, 1)
+    ]
+    ones = []
+    for s in (0, 1):
+        core_copies[s].wait_recv()
+        size = whole[s] // 2
+        away = base[s] + (1 - first_bit[s]) * size
+        add(acc, away, x_ref, mine + away, [(got_core, away)], size)
+        ones.append(
+            push(
+                acc.at[at(away, size)],
+                got_one.at[at(base[s] // 2, size)],
+                first_peer[s],
+            )
+        )
+        stay = base[s] + first_bit[s] * size
+        add(acc, stay, x_ref, mine + stay, [(got_core, stay)], size)
+    twos = []
+    for s in (0, 1):
+        ones[s].wait_recv()
+        size = whole[s] // 4
+        start = base[s] + first_bit[s] * (whole[s] // 2)
+        away = (1 - second_bit[s]) * size
+        add(acc, start + away, acc, start + away, [(got_one, base[s] // 2 + away)], size)
+        twos.append(
+            push(
+                acc.at[at(start + away, size)],
+                got_two.at[at(base[s] // 4, size)],
+                second_peer[s],
+            )
+        )
+        stay = second_bit[s] * size
+        add(acc, start + stay, acc, start + stay, [(got_one, base[s] // 2 + stay)], size)
+    fars = []
+    for s in (0, 1):
+        twos[s].wait_recv()
+        size = whole[s] // 4
+        start = base[s] + first_bit[s] * (whole[s] // 2) + second_bit[s] * size
+        add(acc, start, acc, start, [(got_two, base[s] // 4)], size)
+        copies = []
+        for k in range(1, FAR):
+            theirs = (z + k) % FAR
+            copies.append(
+                push(
+                    acc.at[at(start + theirs * PIECES[s], PIECES[s])],
+                    got_far.at[at((k - 1) * sum(PIECES) + s * PIECES[0], PIECES[s])],
+                    far_peers[k - 1],
+                )
+            )
+        fars.append(copies)
+    back = []
+    for s in (0, 1):
+        for copy in fars[s]:
+            copy.wait_recv()
+        start = base[s] + first_bit[s] * (whole[s] // 2) + second_bit[s] * (whole[s] // 4)
+        piece = start + z * PIECES[s]
+        add(
+            out_ref,
+            mine + piece,
+            acc,
+            piece,
+            [(got_far, k * sum(PIECES) + s * PIECES[0]) for k in range(FAR - 1)],
+            PIECES[s],
+        )
+        span = at(mine + piece, PIECES[s])
+        back.append([push(out_ref.at[span], out_ref.at[span], peer) for peer in far_peers])
+    two_back = []
+    for s in (0, 1):
+        for copy in back[s]:
+            copy.wait_recv()
+        size = whole[s] // 4
+        start = base[s] + first_bit[s] * (whole[s] // 2) + second_bit[s] * size
+        span = at(mine + start, size)
+        two_back.append(push(out_ref.at[span], out_ref.at[span], second_peer[s]))
+    one_back = []
+    for s in (0, 1):
+        two_back[s].wait_recv()
+        size = whole[s] // 2
+        span = at(mine + base[s] + first_bit[s] * size, size)
+        one_back.append(push(out_ref.at[span], out_ref.at[span], first_peer[s]))
+    core_back = []
+    for s in (0, 1):
+        one_back[s].wait_recv()
+        span = at(mine + base[s], whole[s])
+        core_back.append(push(out_ref.at[span], out_ref.at[span], core_peer))
+    for copy in core_back:
+        copy.wait_recv()
+    for copy in core_copies + ones + twos + fars[0] + fars[1]:
+        copy.wait_send()
+    for copy in back[0] + back[1] + two_back + one_back + core_back:
+        copy.wait_send()
+
+
+def reduce_call(partial):
+    rows, columns = partial.shape
+    assert rows == 8 * FAR * sum(PIECES)
+    copies = 6 + 2 * (FAR - 1) + 6 + 2 * (FAR - 1)
+    kind = partial.dtype
+    return pl.pallas_call(
+        reduce_kernel,
+        in_specs=[pl.BlockSpec(memory_space=pltpu.VMEM)],
+        out_specs=pl.BlockSpec(memory_space=pltpu.VMEM),
+        out_shape=jax.ShapeDtypeStruct(partial.shape, kind),
+        scratch_shapes=[
+            pltpu.VMEM((rows // 2, columns), kind),
+            pltpu.VMEM((rows // 2, columns), kind),
+            pltpu.VMEM((rows // 4, columns), kind),
+            pltpu.VMEM((rows // 8, columns), kind),
+            pltpu.VMEM(((FAR - 1) * sum(PIECES), columns), kind),
+            pltpu.SemaphoreType.DMA((copies,)),
+            pltpu.SemaphoreType.DMA((copies,)),
+        ],
+        compiler_params=pltpu.CompilerParams(
+            collective_id=0, has_side_effects=True, vmem_limit_bytes=40 * 1024 * 1024
+        ),
+    )(partial)
+
+
+def total_gradients(down_term, conv_term, up_term):
+    kids, channels = down_term.shape[0] // down_term.shape[1], down_term.shape[1]
+    offsets = conv_term.shape[0]
+    axes = ("vox", "rep")
+    if lax.axis_size("vox") != 2 * FAR or lax.axis_size("rep") != 4:
+        sums = lax.psum((down_term, conv_term, up_term), axes)
+        return [total.astype(jnp.bfloat16) for total in sums]
+    half = jnp.bfloat16
+    wide = 2 * channels
+    pairs = kids // 2
+    up_rows = pairs * channels
+    row_sets = jnp.concatenate(
+        [conv_term.reshape(-1, channels).astype(half), down_term.astype(half)], 0
+    )
+    left = -(-(offsets + kids) // 2) * channels
+    total_rows = 8 * FAR * sum(PIECES)
+    left_rows = jnp.pad(row_sets[:left], ((0, total_rows - up_rows - left), (0, 0)))
+    right_rows = jnp.pad(
+        row_sets[left:], ((0, total_rows - up_rows - (row_sets.shape[0] - left)), (0, 0))
+    )
+    lower = jnp.concatenate([left_rows, right_rows], 1)
+    ups = [up_term[:, p * wide : (p + 1) * wide].astype(half) for p in range(pairs)]
+    done = reduce_call(jnp.concatenate(ups + [lower], 0))
+    up_total = jnp.concatenate(
+        [done[p * channels : (p + 1) * channels] for p in range(pairs)], 1
+    )
+    rest = done[up_rows : up_rows + left]
+    conv_right = offsets * channels - left
+    conv_total = jnp.concatenate([rest[:, :channels], rest[:conv_right, channels:]], 0)
+    down_total = rest[conv_right : conv_right + kids * channels, channels:]
+    return down_total, conv_total.reshape(offsets, channels, channels), up_total
+
+
 def per_device(
     fine_feats, occupancy, parent, neighbors, cotangent, down_weight, conv_weight, up_weight
 ):
@@ -156,11 +368,11 @@
     rows = rows.astype(jnp.bfloat16)
     up_term = dot(rows[:channels], cot_groups, ((1,), (0,)))
     down_term = dot(grouped, rows[channels:], ((0,), (1,)))
-    total_down, total_conv, total_up = lax.psum((down_term, conv_term, up_term), ("vox", "rep"))
+    total_down, total_conv, total_up = total_gradients(down_term, conv_term, up_term)
     return (
-        total_down.astype(jnp.bfloat16).reshape(8, channels, channels),
-        total_conv.astype(jnp.bfloat16),
-        total_up.astype(jnp.bfloat16).reshape(channels, 8, channels),
+        total_down.reshape(8, channels, channels),
+        total_conv,
+        total_up.reshape(channels, 8, channels),
     )
 
 

time: 285 us -> 214 us (0.75)
  blocking collectives: 144 us -> 0 us
  Pallas kernels: 38.8 us -> 105 us
  waiting for transfers between devices: 17.2 us -> 5.91 us
  other arithmetic: 10.6 us -> 21.3 us
  local copies, waits for them, and re-layouts: 43.4 us -> 46.9 us
  matrix products: 7.92 us -> 11.1 us
    psum x1 -> x0, blocking collectives: 144 us -> none  [per_device(): lax.psum((down_term, conv_term, up_term), ('vox', 'rep'))]
    pallas_call x0 -> x1, Pallas kernels: none -> 65 us  [reduce_call(): pl.pallas_call(reduce_kernel, in_specs=[pl.BlockSpec(memory_space=pltpu.V...]
    ppermute x1, waiting for transfers between devices: 11.4 us -> 0.01 us  [per_device(): before = lax.ppermute(own, 'vox', up)]
    concatenate x0 -> x4, other arithmetic: none -> 4.29 us  [the longest x1 1.93 us: total_gradients(): jnp.concatenate([rest[:, :channels], rest[:conv_right, channels:]], 0)]
    dot_general x10, matrix products: 7.92 us -> 11.1 us  [dot(): lax.dot_general(left, right, (dims, ((), ())), precision=precision, prefe...]
    pad x0 -> x1, other arithmetic: none -> 2.86 us  [total_gradients(): jnp.pad(row_sets[:left], ((0, total_rows - up_rows - left), (0, 0)))]
    convert_element_type x0 -> x1, other arithmetic: none -> 2.86 us  [total_gradients(): conv_term.reshape(-1, channels).astype(half)]
    unnamed x23 -> x46, local copies, waits for them, and re-layouts: 13 us -> 11.6 us
  transfers between devices with their start and end apart: 6 -> 6, of which waited for: 2 -> 2; matrix products, arithmetic and copies ran while one was open for 17% -> 26% of each run, Pallas kernels for 0% -> 0%
where the time goes in v2:
time: 214 us; the launch traced here: 213 us
  Pallas kernels  105 us (49%)
  local copies, waits for them, and re-layouts  46.9 us (22%)
  starting transfers between devices  21.8 us (10%)
  other arithmetic  21.3 us (10%)
  matrix products  11.1 us (5%)
  waiting for transfers between devices  5.91 us (3%)
    pallas_call x1, Pallas kernels, reduce_call(): pl.pallas_call(reduce_kernel, in_specs=[pl.BlockSpec(memory_space=pltpu.V...  65 us
    pallas_call x1, Pallas kernels, conv_call(): pl.pallas_call(conv_kernel, grid=(offsets,), in_specs=[pl.BlockSpec((2 *...  40.3 us
    unnamed x46, local copies, waits for them, and re-layouts  11.6 us
    dot_general x10, matrix products, dot(): lax.dot_general(left, right, (dims, ((), ())), precision=precision, prefe...  11.1 us
    mul x4, local copies, waits for them, and re-layouts, per_device(): grouped = (fine_rows * mask_half).reshape(count, 8 * channels)  7.66 us
    ppermute x1, starting transfers between devices, per_device(): lax.ppermute(near_next, 'vox', up)  6.1 us
    mul x2, local copies, waits for them, and re-layouts, per_device(): cot_groups = (cot_rows * mask_half).reshape(count, 8 * channels)  5.96 us
    all_to_all x1, waiting for transfers between devices, per_device(): got = lax.all_to_all(send, 'vox', split_axis=0, concat_axis=0, tiled=True)  5.78 us
  transfers between devices with their start and end apart: 6, of which 2 were waited for; matrix products, arithmetic and copies ran while one was open for 26% of the time, Pallas kernels for 0%

profile of v2, /device:TPU:0, one launch (start us, length us, event | category | flops | bytes accessed | tf_op | source)
XLA Modules:
  0.0 213.3 jit_solution(4812291139199617538)
XLA Ops:
  0.6 1.5 fusion.17
  2.2 1.3 collective-permute-start.3
  3.5 6.1 %collective-permute-start.2 = (s32[27,512]{1,0:T(8,128)}, s32[27,512]{1,0:T(8,128)}, u32[]{:S(2)}, u32[]{:S(2)}) collective-permute-start(s32[27,512]{1,0:T(8,128)} %get-tuple-element.19), channel_id=1, source_target_pairs={{0,4},{4,8},{8,12},{12,16},{16,20},{20,24},{24,28},{1,5},{5,9},{9,... | collective-permute-start | bytes 165896 | tf_op jit(solution)/shard_map/ppermute | solution.py:317
  9.6 0.7 broadcast_compare_fusion
  10.3 1.1 reduce-window.6
  11.4 0.2 slice_reduce_fusion
  11.7 0.7 broadcast_compare_fusion.1
  12.5 0.7 compare_select_fusion.4
  13.3 0.5 convert_element_type.67
  13.8 0.8 convert_reduce_fusion
  14.6 3.8 %broadcast_multiply_fusion.1 = (bf16[1,4096,192]{1,2,0:T(8,128)(2,1)}, bf16[1,4096,192]{1,2,0:T(8,128)(2,1)}) fusion(bf16[1,4096,192]{1,2,0:T(8,128)(2,1)} %param.8, bf16[4096]{0:T(1024)(128)(2,1)S(1)} %convert_reduce_fusion, bf16[1,4096,192]{1,2,0:T(8,128)(2,1)} %param.12), kind=kLoop, calls=%fused_computation.19 | loop fusion | flops 1572864 | bytes 6299648 | tf_op jit(solution)/shard_map/mul | solution.py:335
  18.4 3.1 %copy.50 = bf16[1,4096,192]{2,1,0:T(8,128)(2,1)S(1)} copy(bf16[1,4096,192]{1,2,0:T(8,128)(2,1)} %get-tuple-element.21) | data formatting | bytes 3145728 | tf_op jit(solution)/shard_map/mul | solution.py:336
  21.5 2.8 %mul.54 = bf16[512,1536]{1,0:T(8,128)(2,1)} reshape(bf16[1,4096,192]{2,1,0:T(8,128)(2,1)S(1)} %copy.50) | data formatting | bytes 3145728 | tf_op jit(solution)/shard_map/mul | solution.py:336
  24.3 1.8 reshape.224
  26.2 3.2 %copy.49 = bf16[1,4096,192]{2,1,0:T(8,128)(2,1)S(1)} copy(bf16[1,4096,192]{1,2,0:T(8,128)(2,1)} %get-tuple-element.20) | data formatting | bytes 3145728 | tf_op jit(solution)/shard_map/mul | solution.py:335
  29.3 2.8 %mul.52 = bf16[512,1536]{1,0:T(8,128)(2,1)} reshape(bf16[1,4096,192]{2,1,0:T(8,128)(2,1)S(1)} %copy.49) | data formatting | bytes 3145728 | tf_op jit(solution)/shard_map/mul | solution.py:335
  32.1 2.2 %fusion.38 = f32[512,192]{0,1:T(8,128)S(1)} fusion(bf16[512,1536]{1,0:T(8,128)(2,1)} %mul.54, bf16[192,1536]{1,0:T(8,128)(2,1)S(1)} %reshape.224), kind=kOutput, calls=%fused_computation.91 | convolution fusion | flops 301989888 | bytes 2555904 | tf_op jit(solution)/shard_map/dot_general | solution.py:12
  34.3 0.7 fusion.37
  35.0 0.4 fusion.7
  35.5 0.6 reshape.226
  36.2 5.6 %all-to-all-start = ((f32[8,2,512]{2,1,0:T(2,128)}), f32[8,2,512]{2,1,0:T(2,128)S(1)}, u32[]{:S(2)}, u32[]{:S(2)}) async-start(f32[8,2,512]{2,1,0:T(2,128)} %reshape.226), calls=%async_computation | async-start | bytes 65536 | tf_op jit(solution)/shard_map/all_to_all | solution.py:343
  41.8 0.9 fusion.6
  42.7 5.8 %all-to-all-done = f32[8,2,512]{2,1,0:T(2,128)S(1)} async-done(((f32[8,2,512]{2,1,0:T(2,128)}), f32[8,2,512]{2,1,0:T(2,128)S(1)}, u32[]{:S(2)}, u32[]{:S(2)}) %all-to-all-start) | async-done | bytes 32800 | tf_op jit(solution)/shard_map/all_to_all | solution.py:343
  48.6 0.5 convolution_add_fusion.1.wide
  49.3 0.8 pad_maximum_fusion.5.own
  50.1 3.1 %collective-permute-start = (bf16[384,512]{1,0:T(8,128)(2,1)}, bf16[384,512]{1,0:T(8,128)(2,1)}, u32[]{:S(2)}, u32[]{:S(2)}) collective-permute-start(bf16[384,512]{1,0:T(8,128)(2,1)} %pad_maximum_fusion.5.own), channel_id=1, source_target_pairs={{0,4},{4,8},{8,12},{12,16},{16,20},{20,24},{24,28},{1,5},{5,9},{9,... | collective-permute-start | bytes 1179656 | tf_op jit(solution)/shard_map/ppermute | solution.py:353
  53.2 1.5 collective-permute-start.1
  54.8 0.2 convert_element_type.71
  55.0 3.2 %copy.57 = bf16[1,4096,192]{2,1,0:T(8,128)(2,1)S(1)} copy(bf16[1,4096,192]{1,2,0:T(8,128)(2,1)} %param.8) | data formatting | bytes 3145728 | tf_op args[0]
  58.1 3.8 %copy.54 = bf16[1,4096,192]{2,1,0:T(8,128)(2,1)} copy(bf16[1,4096,192]{1,2,0:T(8,128)(2,1)} %param.12) | data formatting | bytes 3145728 | tf_op args[4]
  62.0 0.7 copy.53
  62.7 2.8 %squeeze.17 = bf16[512,1536]{1,0:T(8,128)(2,1)} reshape(bf16[1,4096,192]{2,1,0:T(8,128)(2,1)S(1)} %copy.57) | data formatting | bytes 3145728 | tf_op jit(solution)/shard_map/squeeze | solution.py:301
  65.5 2.6 %copy.58 = bf16[512,1536]{0,1:T(8,128)(2,1)} copy(bf16[512,1536]{1,0:T(8,128)(2,1)} %squeeze.17) | data formatting | bytes 3145728 | tf_op jit(solution)/shard_map/squeeze | solution.py:301
  68.2 1.1 copy-done.5
  69.4 1.6 copy.56
  71.0 4.5 %squeeze.16 = bf16[512,1536]{1,0:T(8,128)(2,1)} reshape(bf16[1,4096,192]{2,1,0:T(8,128)(2,1)} %copy.54) | data formatting | bytes 3145728 | tf_op jit(solution)/shard_map/squeeze | solution.py:305
  75.5 0.9 copy.52
  76.4 0.9 concatenate.46
  77.3 0.2 fusion.13.ids_in
  77.5 40.3 %shard_map.103 = (f32[27,192,192]{2,1,0:T(8,128)}, bf16[384,512]{1,0:T(8,128)(2,1)S(1)}) custom-call(bf16[384,512]{1,0:T(8,128)(2,1)} %collective-permute-done.before, bf16[384,512]{1,0:T(8,128)(2,1)} %pad_maximum_fusion.5.own, bf16[384,512]{1,0:T(8,128)(2,1)} %collective-permute-done.1.after, f32[384,512]{1,0:T(8,128)S(1)} %convolution_add_fusion.1.wide, ...), custom_call_target="tpu_custom_call" | custom-call | tf_op jit(solution)/shard_map/pallas_call | solution.py:64
  117.8 0.7 copy-done.3
  118.5 0.2 convolution_convert_fusion.2
  118.8 0.6 reshape.228
  119.4 4.2 %all-to-all-start.1 = ((bf16[8,2,384]{2,1,0:T(2,128)(2,1)}), bf16[8,2,384]{2,1,0:T(2,128)(2,1)S(1)}, u32[]{:S(2)}, u32[]{:S(2)}) async-start(bf16[8,2,384]{2,1,0:T(2,128)(2,1)} %reshape.228), calls=%async_computation.1 | async-start | bytes 24576 | tf_op jit(solution)/shard_map/all_to_all | solution.py:358
  123.6 2.9 %convert_element_type.72 = bf16[27,192,192]{2,1,0:T(8,128)(2,1)S(1)} convert(f32[27,192,192]{2,1,0:T(8,128)} %get-tuple-element.6) | non-fusion elementwise | flops 995328 | bytes 5971968 | tf_op jit(solution)/shard_map/convert_element_type | solution.py:277
  126.5 0.1 slice.105
  126.6 0.5 copy-done.18
  127.1 2.9 %bitcast_select_fusion = bf16[3840,192]{1,0:T(8,128)(2,1)} fusion(bf16[20,192,192]{2,1,0:T(8,128)(2,1)S(1)} %slice.105, pred[3840]{0:T(1024)(128)(4,1)S(1)} %copy-done.18), kind=kLoop, calls=%fused_computation.8 | loop fusion | flops 737280 | bytes 2952960 | tf_op jit(solution)/shard_map/jit(_pad)/pad | solution.py:281
  130.0 0.1 all-to-all-done.1
  130.2 0.3 fusion.20
  130.5 0.4 fusion.5
  130.9 0.7 copy-done.9
  131.7 2.9 %convolution_convert_fusion = bf16[1536,192]{0,1:T(8,128)(2,1)} fusion(bf16[512,1536]{0,1:T(8,128)(2,1)} %copy.58, bf16[512,1536]{0,1:T(8,128)(2,1)S(1)} %bitcast.36, bf16[384,512]{1,0:T(8,128)(2,1)S(1)} %fusion.5), kind=kOutput, calls=%fused_computation.5 | convolution fusion | flops 303071232 | bytes 3932160 | tf_op jit(solution)/shard_map/dot_general | solution.py:12
  134.6 1.3 copy.59
  135.9 2.5 %convolution_convert_fusion.1 = bf16[192,1536]{1,0:T(8,128)(2,1)S(1)} fusion(bf16[512,1536]{1,0:T(8,128)(2,1)} %squeeze.16, bf16[512,1536]{1,0:T(8,128)(2,1)} %copy.56, bf16[384,512]{1,0:T(8,128)(2,1)} %copy-done.9), kind=kOutput, calls=%fused_computation.6 | convolution fusion | flops 303071232 | bytes 3932160 | tf_op jit(solution)/shard_map/dot_general | solution.py:12
  138.6 0.3 fusion.2
  138.9 1.2 copy-done.7
  140.1 1.2 maximum_dynamic-update-slice_fusion.x_ref
  141.3 65.0 %shard_map.104 = bf16[4608,384]{1,0:T(8,128)(2,1)S(1)} custom-call(bf16[4608,384]{1,0:T(8,128)(2,1)S(1)} %maximum_dynamic-update-slice_fusion.x_ref), custom_call_target="tpu_custom_call" | custom-call | tf_op jit(solution)/shard_map/pallas_call | solution.py:245
  206.5 0.4 slice.90
  206.8 1.2 slice.88
  208.1 0.9 pad_maximum_fusion.4
  208.9 2.5 %reshape.233 = bf16[192,8,192]{2,1,0:T(8,128)(2,1)} reshape(bf16[192,1536]{1,0:T(8,128)(2,1)} %pad_maximum_fusion.4) | data formatting | bytes 1179648 | tf_op jit(solution)/shard_map/reshape | solution.py:375
  211.4 1.9 pad_maximum_fusion
  (61 shorter events, 1.3 us)
Async XLA Ops:
  0.6 33.6 %copy-start = (bf16[8,192,192]{2,1,0:T(8,128)(2,1)S(1)}, bf16[8,192,192]{2,1,0:T(8,128)(2,1)}, u32[]{:S(2)}) copy-start(bf16[8,192,192]{2,1,0:T(8,128)(2,1)} %param.13) | copy-start | bytes 1769476
  2.2 74.2 %collective-permute-start.3 = (s32[27,512]{1,0:T(8,128)}, s32[27,512]{1,0:T(8,128)}, u32[]{:S(2)}, u32[]{:S(2)}) collective-permute-start(s32[27,512]{1,0:T(8,128)} %get-tuple-element.19), channel_id=1, source_target_pairs={{4,0},{8,4},{12,8},{16,12},{20,16},{24,20},{28,24},{5,1},{9,5},{13... | collective-permute-start | bytes 165896 | tf_op jit(solution)/shard_map/ppermute | solution.py:317
  3.5 72.0 %collective-permute-start.2 = (s32[27,512]{1,0:T(8,128)}, s32[27,512]{1,0:T(8,128)}, u32[]{:S(2)}, u32[]{:S(2)}) collective-permute-start(s32[27,512]{1,0:T(8,128)} %get-tuple-element.19), channel_id=1, source_target_pairs={{0,4},{4,8},{8,12},{12,16},{16,20},{20,24},{24,28},{1,5},{5,9},{9,... | collective-permute-start | bytes 165896 | tf_op jit(solution)/shard_map/ppermute | solution.py:317
  13.2 21.8 %copy-start.12 = (s32[1,512]{1,0:T(1,128)}, s32[1,512]{1,0:T(1,128)S(1)}, u32[]{:S(2)}) copy-start(s32[1,512]{1,0:T(1,128)S(1)} %get-tuple-element.7) | copy-start | bytes 6148
  13.2 28.6 %copy-start.14 = (s32[1,512]{1,0:T(1,128)}, s32[1,512]{1,0:T(1,128)S(1)}, u32[]{:S(2)}) copy-start(s32[1,512]{1,0:T(1,128)S(1)} %get-tuple-element.23) | copy-start | bytes 6148
  32.1 2.2 %copy-start.8 = (bf16[512,1536]{1,0:T(8,128)(2,1)S(1)}, bf16[512,1536]{1,0:T(8,128)(2,1)}, u32[]{:S(2)}) copy-start(bf16[512,1536]{1,0:T(8,128)(2,1)} %mul.52) | copy-start | bytes 4718596
  34.3 1.2 copy-start.19
  36.2 12.3 %all-to-all-start = ((f32[8,2,512]{2,1,0:T(2,128)}), f32[8,2,512]{2,1,0:T(2,128)S(1)}, u32[]{:S(2)}, u32[]{:S(2)}) async-start(f32[8,2,512]{2,1,0:T(2,128)} %reshape.226), calls=%async_computation | async-start | bytes 65536 | tf_op jit(solution)/shard_map/all_to_all | solution.py:343
  42.7 12.0 %copy-start.10 = (s32[1,27,512]{2,0,1:T(1,128)S(1)}, s32[1,27,512]{2,0,1:T(1,128)}, u32[]{:S(2)}) copy-start(s32[1,27,512]{2,0,1:T(1,128)} %param.11) | copy-start | bytes 165892
  48.6 4.6 %copy-start.16 = (s32[16]{0:T(128)}, s32[16]{0:T(128)S(1)}, u32[]{:S(2)}) copy-start(s32[16]{0:T(128)S(1)} %fusion.29) | copy-start | bytes 196
  50.1 27.4 %collective-permute-start = (bf16[384,512]{1,0:T(8,128)(2,1)}, bf16[384,512]{1,0:T(8,128)(2,1)}, u32[]{:S(2)}, u32[]{:S(2)}) collective-permute-start(bf16[384,512]{1,0:T(8,128)(2,1)} %pad_maximum_fusion.5.own), channel_id=1, source_target_pairs={{0,4},{4,8},{8,12},{12,16},{16,20},{20,24},{24,28},{1,5},{5,9},{9,... | collective-permute-start | bytes 1179656 | tf_op jit(solution)/shard_map/ppermute | solution.py:353
  53.2 24.2 %collective-permute-start.1 = (bf16[384,512]{1,0:T(8,128)(2,1)}, bf16[384,512]{1,0:T(8,128)(2,1)}, u32[]{:S(2)}, u32[]{:S(2)}) collective-permute-start(bf16[384,512]{1,0:T(8,128)(2,1)} %pad_maximum_fusion.5.own), channel_id=1, source_target_pairs={{4,0},{8,4},{12,8},{16,12},{20,16},{24,20},{28,24},{5,1},{9,5},{13... | collective-permute-start | bytes 1179656 | tf_op jit(solution)/shard_map/ppermute | solution.py:354
  68.2 1.2 copy-start.5
  71.0 6.3 %copy-start.11 = (s32[27,1,512]{2,1,0:T(1,128)S(1)}, s32[27,1,512]{2,1,0:T(1,128)}, u32[]{:S(2)}) copy-start(s32[27,1,512]{2,1,0:T(1,128)} %copy.53) | copy-start | bytes 165892
  71.0 6.5 %copy-start.2 = (bf16[27,192,192]{2,1,0:T(8,128)(2,1)S(1)}, bf16[27,192,192]{2,1,0:T(8,128)(2,1)}, u32[]{:S(2)}) copy-start(bf16[27,192,192]{2,1,0:T(8,128)(2,1)} %weight.1) | copy-start | bytes 5971972
  77.5 41.1 %copy-start.17 = (s32[16]{0:T(128)S(1)}, s32[16]{0:T(128)}, u32[]{:S(2)}) copy-start(s32[16]{0:T(128)} %copy-done.16) | copy-start | bytes 196
  117.8 0.7 copy-start.3
  119.4 10.7 %all-to-all-start.1 = ((bf16[8,2,384]{2,1,0:T(2,128)(2,1)}), bf16[8,2,384]{2,1,0:T(2,128)(2,1)S(1)}, u32[]{:S(2)}, u32[]{:S(2)}) async-start(bf16[8,2,384]{2,1,0:T(2,128)(2,1)} %reshape.228), calls=%async_computation.1 | async-start | bytes 24576 | tf_op jit(solution)/shard_map/all_to_all | solution.py:358
  126.4 0.7 copy-start.18
  127.1 3.0 %copy-start.13 = (s32[1,512]{1,0:T(1,128)S(1)}, s32[1,512]{1,0:T(1,128)}, u32[]{:S(2)}) copy-start(s32[1,512]{1,0:T(1,128)} %copy-done.12) | copy-start | bytes 6148
  127.1 3.3 %copy-start.4 = (bf16[384,512]{1,0:T(8,128)(2,1)S(1)}, bf16[384,512]{1,0:T(8,128)(2,1)}, u32[]{:S(2)}) copy-start(bf16[384,512]{1,0:T(8,128)(2,1)} %copy-done.3) | copy-start | bytes 1179652
  127.1 3.3 %copy-start.15 = (s32[1,512]{1,0:T(1,128)S(1)}, s32[1,512]{1,0:T(1,128)}, u32[]{:S(2)}) copy-start(s32[1,512]{1,0:T(1,128)} %copy-done.14) | copy-start | bytes 6148
  130.2 1.5 copy-start.6
  130.9 0.7 copy-start.9
  138.5 1.5 copy-start.7
  208.9 4.4 %copy-start.1 = (bf16[8,192,192]{2,1,0:T(8,128)(2,1)S(1)}, bf16[8,192,192]{2,1,0:T(8,128)(2,1)}, u32[]{:S(2)}) copy-start(bf16[8,192,192]{2,1,0:T(8,128)(2,1)} %param.13) | copy-start | bytes 1769476

commit v3 on v2

--- a/solution.py
+++ b/solution.py
@@ -1,3 +1,5 @@
+import functools
+
 import jax
 import jax.numpy as jnp
 from jax import lax
@@ -42,7 +44,16 @@
     acc_down[...] = spread
     gathered = gathered.astype(jnp.bfloat16)
     acc_up[...] += dot(weight_here, gathered, ((0,), (0,)))
-    term_ref[0] = dot(gathered, own[channels:, :], ((1,), (1,)))
+    term = dot(gathered, own[channels:, :], ((1,), (1,))).astype(term_ref.dtype)
+
+    @pl.when(step % 2 == 0)
+    def _():
+        term_ref[:, :channels] = term
+        term_ref[:, channels:] = jnp.zeros_like(term)
+
+    @pl.when(step % 2 == 1)
+    def _():
+        term_ref[:, channels:] = term
 
     @pl.when(step == pl.num_programs(0) - 1)
     def _():
@@ -56,7 +67,7 @@
         )
 
 
-def conv_call(before, own, after, wide, ids_out, ids_in, conv_weight):
+def conv_call(packed_rows, before, own, after, wide, ids_out, ids_in, conv_weight):
     offsets, channels = conv_weight.shape[:2]
     count = own.shape[1]
     whole = lambda j: (0, 0)
@@ -71,11 +82,13 @@
             pl.BlockSpec((1, channels, channels), each),
         ],
         out_specs=[
-            pl.BlockSpec((1, channels, channels), each),
+            pl.BlockSpec((channels, 2 * channels), lambda j: (j // 2, 0)),
             pl.BlockSpec((2 * channels, count), whole),
         ],
         out_shape=[
-            jax.ShapeDtypeStruct((offsets, channels, channels), jnp.float32),
+            jax.ShapeDtypeStruct(
+                (packed_rows, 2 * channels), jnp.bfloat16 if has_plan() else jnp.float32
+            ),
             jax.ShapeDtypeStruct((2 * channels, count), jnp.bfloat16),
         ],
         scratch_shapes=[pltpu.VMEM((channels, count), jnp.float32)] * 2,
@@ -124,15 +137,17 @@
         return pl.ds(pl.multiple_of(start, UNIT), size)
 
     def add(target, target_at, left, left_at, others, size):
+        chunk = 80 if size % 80 == 0 else 64
+
         def body(i, carry):
-            step = i * UNIT
-            total = left[at(left_at + step, UNIT), :].astype(jnp.float32)
+            step = i * chunk
+            total = left[at(left_at + step, chunk), :].astype(jnp.float32)
             for ref, ref_at in others:
-                total += ref[at(ref_at + step, UNIT), :].astype(jnp.float32)
-            target[at(target_at + step, UNIT), :] = total.astype(target.dtype)
+                total += ref[at(ref_at + step, chunk), :].astype(jnp.float32)
+            target[at(target_at + step, chunk), :] = total.astype(target.dtype)
             return carry
 
-        lax.fori_loop(0, size // UNIT, body, 0)
+        lax.fori_loop(0, size // chunk, body, 0)
 
     half = 4 * FAR * sum(PIECES)
     base = [0, 4 * FAR * PIECES[0]]
@@ -262,37 +277,96 @@
     )(partial)
 
 
-def total_gradients(down_term, conv_term, up_term):
-    kids, channels = down_term.shape[0] // down_term.shape[1], down_term.shape[1]
-    offsets = conv_term.shape[0]
-    axes = ("vox", "rep")
-    if lax.axis_size("vox") != 2 * FAR or lax.axis_size("rep") != 4:
-        sums = lax.psum((down_term, conv_term, up_term), axes)
-        return [total.astype(jnp.bfloat16) for total in sums]
-    half = jnp.bfloat16
-    wide = 2 * channels
-    pairs = kids // 2
-    up_rows = pairs * channels
-    row_sets = jnp.concatenate(
-        [conv_term.reshape(-1, channels).astype(half), down_term.astype(half)], 0
-    )
-    left = -(-(offsets + kids) // 2) * channels
-    total_rows = 8 * FAR * sum(PIECES)
-    left_rows = jnp.pad(row_sets[:left], ((0, total_rows - up_rows - left), (0, 0)))
-    right_rows = jnp.pad(
-        row_sets[left:], ((0, total_rows - up_rows - (row_sets.shape[0] - left)), (0, 0))
-    )
-    lower = jnp.concatenate([left_rows, right_rows], 1)
-    ups = [up_term[:, p * wide : (p + 1) * wide].astype(half) for p in range(pairs)]
-    done = reduce_call(jnp.concatenate(ups + [lower], 0))
-    up_total = jnp.concatenate(
-        [done[p * channels : (p + 1) * channels] for p in range(pairs)], 1
-    )
-    rest = done[up_rows : up_rows + left]
-    conv_right = offsets * channels - left
-    conv_total = jnp.concatenate([rest[:, :channels], rest[:conv_right, channels:]], 0)
-    down_total = rest[conv_right : conv_right + kids * channels, channels:]
-    return down_total, conv_total.reshape(offsets, channels, channels), up_total
+def group_kernel(fine, cot, occupied, down_w, up_w, grouped, cot_groups, values, *wide):
+    kids, count, channels = grouped.shape
+    cuts = [(c, min(c + 128, channels)) for c in range(0, channels, 128)]
+    wide_fine, wide_cot = wide[: len(cuts)], wide[len(cuts) :]
+    for source, parts in ((fine, wide_fine), (cot, wide_cot)):
+        for part, (low, high) in zip(parts, cuts):
+            part[:, : high - low] = source[:, low:high].astype(jnp.float32)
+
+    def child(parts, k):
+        pieces = [
+            part[pl.ds(k, count, stride=kids), :][:, : high - low]
+            for part, (low, high) in zip(parts, cuts)
+        ]
+        return jnp.concatenate(pieces, 1)
+
+    pre = jnp.zeros((count, channels), jnp.float32)
+    back = jnp.zeros((count, channels), jnp.float32)
+    for k in range(kids):
+        mask = occupied[:, k : k + 1]
+        rows = (child(wide_fine, k) * mask).astype(jnp.bfloat16)
+        grouped[k] = rows
+        pre += dot(rows, down_w[k], ((1,), (0,)))
+        rows = (child(wide_cot, k) * mask).astype(jnp.bfloat16)
+        cot_groups[k] = rows
+        back += dot(rows, up_w[k], ((1,), (1,)))
+    values[:, :channels] = pre
+    values[:, channels:] = back
+
+
+def group_call(fine, cot, occupied, down_w, up_w):
+    kids, channels = down_w.shape[:2]
+    count = occupied.shape[0]
+    return pl.pallas_call(
+        group_kernel,
+        in_specs=[pl.BlockSpec(memory_space=pltpu.VMEM)] * 5,
+        out_specs=[pl.BlockSpec(memory_space=pltpu.VMEM)] * 3,
+        out_shape=[
+            jax.ShapeDtypeStruct((kids, count, channels), jnp.bfloat16),
+            jax.ShapeDtypeStruct((kids, count, channels), jnp.bfloat16),
+            jax.ShapeDtypeStruct((count, 2 * channels), jnp.float32),
+        ],
+        scratch_shapes=[pltpu.VMEM((fine.shape[0], 128), jnp.float32)]
+        * (2 * (-(-channels // 128))),
+        compiler_params=pltpu.CompilerParams(vmem_limit_bytes=40 * 1024 * 1024),
+    )(fine, cot, occupied, down_w, up_w)
+
+
+def outer_kernel(kids, up_rows, down_rows, cot_groups, grouped, packed, out):
+    del packed
+    channels = up_rows.shape[0]
+    step = pl.program_id(0)
+
+    @pl.when(step < kids)
+    def _():
+        out[:, :channels] = dot(up_rows[...], cot_groups[0], ((1,), (0,))).astype(out.dtype)
+        out[:, channels:] = dot(grouped[0], down_rows[...], ((0,), (0,))).astype(out.dtype)
+
+    @pl.when(step >= kids)
+    def _():
+        out[...] = jnp.zeros_like(out)
+
+
+def outer_call(taken, up_rows, down_rows, cot_groups, grouped, packed):
+    kids, count, channels = grouped.shape
+    blocks = packed.shape[0] // channels
+    kid = lambda p: (jnp.minimum(p, kids - 1), 0, 0)
+    return pl.pallas_call(
+        functools.partial(outer_kernel, kids),
+        grid=(blocks - taken,),
+        in_specs=[
+            pl.BlockSpec((channels, count), lambda p: (0, 0)),
+            pl.BlockSpec((count, channels), lambda p: (0, 0)),
+            pl.BlockSpec((1, count, channels), kid),
+            pl.BlockSpec((1, count, channels), kid),
+            pl.BlockSpec(memory_space=pl.ANY),
+        ],
+        out_specs=pl.BlockSpec((channels, 2 * channels), lambda p: (taken + p, 0)),
+        out_shape=jax.ShapeDtypeStruct(packed.shape, packed.dtype),
+        input_output_aliases={4: 0},
+    )(up_rows, down_rows, cot_groups, grouped, packed)
+
+
+def has_plan():
+    return lax.axis_size("vox") == 2 * FAR and lax.axis_size("rep") == 4
+
+
+def total_gradients(packed):
+    if has_plan():
+        return reduce_call(packed)
+    return lax.psum(packed, ("vox", "rep")).astype(jnp.bfloat16)
 
 
 def per_device(
@@ -331,12 +405,15 @@
     place = jnp.arange(slots, dtype=jnp.int32)[:, None] == dest[None, :]
     send_ids = jnp.sum(jnp.where(place, local_id[None, :] + 1, 0), axis=1)
 
-    mask_half = occupied.astype(jnp.bfloat16)[:, None]
-    grouped = (fine_rows * mask_half).reshape(count, 8 * channels)
-    cot_groups = (cot_rows * mask_half).reshape(count, 8 * channels)
-    pre_groups = dot(grouped, down_weight.reshape(8 * channels, channels), ((1,), (0,)))
-    back_groups = dot(cot_groups, up_weight.reshape(channels, 8 * channels), ((1,), (1,)))
-    values = jnp.concatenate([pre_groups, back_groups], 1)
+    kids = down_weight.shape[0]
+    up_first = jnp.transpose(up_weight, (1, 0, 2))
+    grouped, cot_groups, values = group_call(
+        fine_rows,
+        cot_rows,
+        occupied.reshape(count, kids).astype(jnp.float32),
+        down_weight,
+        up_first,
+    )
     send = dot(place.astype(jnp.float32), values, ((1,), (0,)), exact)
     tail = jnp.broadcast_to(send_ids.astype(jnp.float32)[:, None], (slots, 128))
     send = jnp.concatenate([send, tail], 1).reshape(vox_count, CAP, 2 * channels + 128)
@@ -352,7 +429,10 @@
     own = jnp.concatenate([jax.nn.silu(wide[:channels]), wide[channels:]], 0).astype(jnp.bfloat16)
     before = lax.ppermute(own, "vox", up)
     after = lax.ppermute(own, "vox", down)
-    conv_term, both = conv_call(before, own, after, wide, ids_out, ids_in, conv_weight)
+    offsets = conv_weight.shape[0]
+    taken = (offsets + 1) // 2
+    packed_rows = 8 * FAR * sum(PIECES)
+    packed, both = conv_call(packed_rows, before, own, after, wide, ids_out, ids_in, conv_weight)
 
     outgoing = dot(arrived.astype(jnp.bfloat16), both, ((0,), (1,))).astype(jnp.bfloat16)
     returned = lax.all_to_all(
@@ -362,17 +442,31 @@
         concat_axis=0,
         tiled=True,
     ).reshape(slots, 2 * channels)
-    rows = dot(both, keep.astype(jnp.bfloat16), ((1,), (0,))) + dot(
-        returned, place.astype(jnp.bfloat16), ((0,), (0,))
-    )
-    rows = rows.astype(jnp.bfloat16)
-    up_term = dot(rows[:channels], cot_groups, ((1,), (0,)))
-    down_term = dot(grouped, rows[channels:], ((0,), (1,)))
-    total_down, total_conv, total_up = total_gradients(down_term, conv_term, up_term)
+    keep_half, place_half = keep.astype(jnp.bfloat16), place.astype(jnp.bfloat16)
+    up_rows = dot(both[:channels], keep_half, ((1,), (0,))) + dot(
+        returned[:, :channels], place_half, ((0,), (0,))
+    )
+    down_rows = dot(keep_half, both[channels:], ((0,), (1,))) + dot(
+        place_half, returned[:, channels:], ((0,), (0,))
+    )
+    packed = outer_call(
+        taken,
+        up_rows.astype(jnp.bfloat16),
+        down_rows.astype(jnp.bfloat16),
+        cot_groups,
+        grouped,
+        packed,
+    )
+    done = total_gradients(packed)
+    pairs = done[: taken * channels].reshape(taken, channels, 2 * channels)
+    conv_total = jnp.stack([pairs[:, :, :channels], pairs[:, :, channels:]], 1)
+    conv_total = conv_total.reshape(-1, channels, channels)
+    rest = done[taken * channels : (taken + kids) * channels]
+    up_total = rest[:, :channels].reshape(kids, channels, channels)
     return (
-        total_down.reshape(8, channels, channels),
-        total_conv,
-        total_up.reshape(channels, 8, channels),
+        rest[:, channels:].reshape(kids, channels, channels),
+        conv_total[:offsets],
+        jnp.transpose(up_total, (1, 0, 2)),
     )
 
 

time: 214 us -> 203 us (0.949)
  local copies, waits for them, and re-layouts: 46.9 us -> 28.6 us
  other arithmetic: 21.3 us -> 8.19 us
  blocking collectives: 0 us -> 10.5 us
  Pallas kernels: 105 us -> 113 us
  waiting for transfers between devices: 5.91 us -> 13.1 us
  matrix products: 11.1 us -> 7.61 us
  starting transfers between devices: 21.8 us -> 19.6 us
    mul x6 -> x0, local copies, waits for them, and re-layouts: 13.6 us -> none  [the longest x4 7.66 us: per_device(): grouped = (fine_rows * mask_half).reshape(count, 8 * channels)]
    pallas_call x0 -> x2, Pallas kernels: none -> 11 us  [the longest x1 7.91 us: outer_call(): pl.pallas_call(functools.partial(outer_kernel, kids), grid=(blocks - take...]
    all_to_all x0 -> x1, blocking collectives: none -> 10.5 us  [per_device(): lax.all_to_all(outgoing.reshape(vox_count, CAP, 2 * channels), 'vox', spl...]
    squeeze x3 -> x0, local copies, waits for them, and re-layouts: 9.85 us -> none  [the longest x2 5.37 us: per_device(): fine_rows = fine_feats[0]]
    ppermute x1, waiting for transfers between devices: 0.01 us -> 7.32 us  [per_device(): before = lax.ppermute(own, 'vox', up)]
    unnamed x46 -> x35, local copies, waits for them, and re-layouts: 11.6 us -> 18.5 us
    pallas_call x1, Pallas kernels: 65 us -> 60.4 us  [reduce_call(): pl.pallas_call(reduce_kernel, in_specs=[pl.BlockSpec(memory_space=pltpu.V...]
    concatenate x4 -> x0, other arithmetic: 4.29 us -> none  [the longest x1 1.93 us: total_gradients(): jnp.concatenate([rest[:, :channels], rest[:conv_right, channels:]], 0)]
  transfers between devices with their start and end apart: 6 -> 5, of which waited for: 2 -> 3; matrix products, arithmetic and copies ran while one was open for 26% -> 12% of each run, Pallas kernels for 0% -> 2%
where the time goes in v3:
time: 203 us; the launch traced here: 202 us
  Pallas kernels  113 us (56%)
  local copies, waits for them, and re-layouts  28.6 us (14%)
  starting transfers between devices  19.6 us (10%)
  waiting for transfers between devices  13.1 us (6%)
  blocking collectives  10.5 us (5%)
  other arithmetic  8.19 us (4%)
  matrix products  7.61 us (4%)
    pallas_call x1, Pallas kernels, reduce_call(): pl.pallas_call(reduce_kernel, in_specs=[pl.BlockSpec(memory_space=pltpu.V...  60.4 us
    pallas_call x1, Pallas kernels, conv_call(): pl.pallas_call(conv_kernel, grid=(offsets,), in_specs=[pl.BlockSpec((2 *...  42 us
    unnamed x35, local copies, waits for them, and re-layouts  18.5 us
    all_to_all x1, blocking collectives, per_device(): lax.all_to_all(outgoing.reshape(vox_count, CAP, 2 * channels), 'vox', spl...  10.5 us
    pallas_call x1, Pallas kernels, outer_call(): pl.pallas_call(functools.partial(outer_kernel, kids), grid=(blocks - take...  7.91 us
    dot_general x8, matrix products, dot(): lax.dot_general(left, right, (dims, ((), ())), precision=precision, prefe...  7.61 us
    ppermute x1, waiting for transfers between devices, per_device(): before = lax.ppermute(own, 'vox', up)  7.32 us
    ppermute x1, starting transfers between devices, per_device(): lax.ppermute(near_next, 'vox', up)  6.11 us
  transfers between devices with their start and end apart: 5, of which 3 were waited for; matrix products, arithmetic and copies ran while one was open for 12% of the time, Pallas kernels for 2%

profile of v3, /device:TPU:0, one launch (start us, length us, event | category | flops | bytes accessed | tf_op | source)
XLA Modules:
  0.0 202.0 jit_solution(4595617012259532353)
XLA Ops:
  0.6 1.5 fusion.12
  2.1 1.3 collective-permute-start.3
  3.4 6.1 %collective-permute-start.2 = (s32[27,512]{1,0:T(8,128)}, s32[27,512]{1,0:T(8,128)}, u32[]{:S(2)}, u32[]{:S(2)}) collective-permute-start(s32[27,512]{1,0:T(8,128)} %get-tuple-element.26), channel_id=1, source_target_pairs={{0,4},{4,8},{8,12},{12,16},{16,20},{20,24},{24,28},{1,5},{5,9},{9,... | collective-permute-start | bytes 165896 | tf_op jit(solution)/shard_map/ppermute | solution.py:391
  9.5 0.7 broadcast_add_fusion
  10.2 0.7 broadcast_compare_fusion.1
  10.9 0.7 broadcast_compare_fusion
  11.6 0.7 compare_select_fusion.5
  12.3 1.1 reduce-window.6
  13.5 0.2 slice_reduce_fusion
  13.7 0.1 fusion.19
  13.8 0.1 select_reduce_fusion
  14.0 0.8 convert_reduce_fusion
  14.7 0.2 convert_element_type.42.occupied
  14.9 2.2 %copy.70 = bf16[192,8,192]{2,0,1:T(8,128)(2,1)} copy(bf16[192,8,192]{2,1,0:T(8,128)(2,1)} %param.15) | data formatting | bytes 1179648 | tf_op args[7]
  17.1 3.1 %copy.53 = bf16[1,4096,192]{2,1,0:T(8,128)(2,1)S(1)} copy(bf16[1,4096,192]{1,2,0:T(8,128)(2,1)} %param.8) | data formatting | bytes 3145728 | tf_op args[0]
  20.2 3.8 %copy.54 = bf16[1,4096,192]{2,1,0:T(8,128)(2,1)} copy(bf16[1,4096,192]{1,2,0:T(8,128)(2,1)} %param.12) | data formatting | bytes 3145728 | tf_op args[4]
  24.1 1.6 copy-done.1
  25.6 1.1 copy-done.2
  26.8 1.1 copy-done.6
  27.9 3.1 %shard_map.103 = (bf16[8,512,192]{2,1,0:T(8,128)(2,1)S(1)}, bf16[8,512,192]{2,1,0:T(8,128)(2,1)S(1)}, f32[512,384]{1,0:T(8,128)S(1)}) custom-call(bf16[4096,192]{1,0:T(8,128)(2,1)S(1)} %bitcast.38, bf16[4096,192]{1,0:T(8,128)(2,1)S(1)} %bitcast.39, f32[512,8]{1,0:T(8,128)S(1)} %convert_element_type.42.occupied, bf16[8,192,192]{2,1,0:T(8,128)(2,1)S(1)} %copy-done.6, ...), custom_call_target="tpu_custom_call" | custom-call | tf_op jit(solution)/shard_map/pallas_call | solution.py:312
  31.0 1.3 copy-done.4
  32.4 1.3 copy-done.5
  33.7 0.4 fusion.17
  34.1 0.1 broadcast_in_dim.45
  34.1 0.6 reshape.191
  34.8 5.6 %all-to-all-start = ((f32[8,2,512]{2,1,0:T(2,128)}), f32[8,2,512]{2,1,0:T(2,128)S(1)}, u32[]{:S(2)}, u32[]{:S(2)}) async-start(f32[8,2,512]{2,1,0:T(2,128)} %reshape.191), calls=%async_computation | async-start | bytes 65536 | tf_op jit(solution)/shard_map/all_to_all | solution.py:420
  40.4 2.3 %fusion.1 = f32[384,512]{1,0:T(8,128)} fusion(f32[512,384]{1,0:T(8,128)S(1)} %get-tuple-element.8, s32[512]{0:T(512)S(1)} %bitcast.52), kind=kOutput, calls=%fused_computation.9 | convolution fusion | flops 1208221696 | bytes 1574912 | tf_op jit(solution)/shard_map/dot_general | solution.py:14
  42.7 4.3 %all-to-all-done = f32[8,2,512]{2,1,0:T(2,128)S(1)} async-done(((f32[8,2,512]{2,1,0:T(2,128)}), f32[8,2,512]{2,1,0:T(2,128)S(1)}, u32[]{:S(2)}, u32[]{:S(2)}) %all-to-all-start) | async-done | bytes 32800 | tf_op jit(solution)/shard_map/all_to_all | solution.py:420
  47.1 0.0 copy-start.3
  47.1 0.1 fusion.29
  47.2 1.8 convolution_add_fusion.wide
  49.1 0.1 multiply_convert_fusion
  49.2 0.8 pad_maximum_fusion.1.own
  50.0 1.3 collective-permute-start.1
  51.3 5.3 %collective-permute-start = (bf16[384,512]{1,0:T(8,128)(2,1)}, bf16[384,512]{1,0:T(8,128)(2,1)}, u32[]{:S(2)}, u32[]{:S(2)}) collective-permute-start(bf16[384,512]{1,0:T(8,128)(2,1)} %pad_maximum_fusion.1.own), channel_id=1, source_target_pairs={{0,4},{4,8},{8,12},{12,16},{16,20},{20,24},{24,28},{1,5},{5,9},{9,... | collective-permute-start | bytes 1179656 | tf_op jit(solution)/shard_map/ppermute | solution.py:430
  56.6 0.1 fusion.14.ids_out
  56.6 0.9 copy.58
  57.5 0.0 collective-permute-done.2
  57.6 0.9 copy.57
  58.5 0.0 collective-permute-done.3
  58.5 0.9 concatenate.27
  59.4 0.2 fusion.8.ids_in
  59.5 1.5 collective-permute-done.1.after
  61.0 7.3 %collective-permute-done.before = bf16[384,512]{1,0:T(8,128)(2,1)} collective-permute-done((bf16[384,512]{1,0:T(8,128)(2,1)}, bf16[384,512]{1,0:T(8,128)(2,1)}, u32[]{:S(2)}, u32[]{:S(2)}) %collective-permute-start) | collective-permute-done | bytes 393248 | tf_op jit(solution)/shard_map/ppermute | solution.py:430
  68.4 42.0 %shard_map.104 = (bf16[4608,384]{1,0:T(8,128)(2,1)}, bf16[384,512]{1,0:T(8,128)(2,1)S(1)}) custom-call(bf16[384,512]{1,0:T(8,128)(2,1)} %collective-permute-done.before, bf16[384,512]{1,0:T(8,128)(2,1)} %pad_maximum_fusion.1.own, bf16[384,512]{1,0:T(8,128)(2,1)} %collective-permute-done.1.after, f32[384,512]{1,0:T(8,128)S(1)} %convolution_add_fusion.wide, ...), custom_call_target="tpu_custom_call" | custom-call | tf_op jit(solution)/shard_map/pallas_call | solution.py:75
  110.4 0.7 copy-done.7
  111.1 0.2 convolution_convert_fusion
  111.4 10.5 %all_to_all.10 = bf16[8,2,384]{2,1,0:T(2,128)(2,1)S(1)} all-to-all(bf16[8,2,384]{2,1,0:T(2,128)(2,1)S(1)} %reshape.193), channel_id=1, replica_groups=mesh['vox'=8,'rep'=4] {'vox'}, dimensions={0} | all-to-all | bytes 24576 | tf_op jit(solution)/shard_map/all_to_all | solution.py:438
  121.9 0.3 fusion.15
  122.2 0.2 fusion.16
  122.5 0.0 copy-done.13
  122.5 1.3 convolution_add_fusion.1
  123.8 0.8 copy.59.down_rows
  124.6 1.0 fusion.up_rows
  125.6 7.9 %shard_map.105.x_ref = bf16[4608,384]{1,0:T(8,128)(2,1)} custom-call(bf16[192,512]{1,0:T(8,128)(2,1)} %fusion.up_rows, bf16[512,192]{1,0:T(8,128)(2,1)} %copy.59.down_rows, bf16[8,512,192]{2,1,0:T(8,128)(2,1)} %copy-done.5, bf16[8,512,192]{2,1,0:T(8,128)(2,1)} %copy-done.4, bf16[4608,384]{1,0:T(8,128)(2,1)} %get-tuple-element.12.packed), custom_call_target="tpu_custom_call", output_to_operand_aliasing={{}: (4, {})} | custom-call | tf_op jit(solution)/shard_map/pallas_call | solution.py:346
  133.6 2.0 copy-done
  135.6 60.4 %shard_map.106 = bf16[4608,384]{1,0:T(8,128)(2,1)S(1)} custom-call(bf16[4608,384]{1,0:T(8,128)(2,1)S(1)} %copy-done), custom_call_target="tpu_custom_call" | custom-call | tf_op jit(solution)/shard_map/pallas_call | solution.py:260
  196.0 1.2 fusion.34
  197.2 0.2 slice.63
  197.5 1.3 copy.69
  198.8 0.7 slice_bitcast_fusion.1
  199.5 0.5 pad_maximum_fusion
  200.0 0.3 copy.60
  200.3 1.7 slice.77
  (33 shorter events, 0.2 us)
Async XLA Ops:
  2.1 56.4 %collective-permute-start.3 = (s32[27,512]{1,0:T(8,128)}, s32[27,512]{1,0:T(8,128)}, u32[]{:S(2)}, u32[]{:S(2)}) collective-permute-start(s32[27,512]{1,0:T(8,128)} %get-tuple-element.26), channel_id=1, source_target_pairs={{4,0},{8,4},{12,8},{16,12},{20,16},{24,20},{28,24},{5,1},{9,5},{13... | collective-permute-start | bytes 165896 | tf_op jit(solution)/shard_map/ppermute | solution.py:391
  3.4 54.2 %collective-permute-start.2 = (s32[27,512]{1,0:T(8,128)}, s32[27,512]{1,0:T(8,128)}, u32[]{:S(2)}, u32[]{:S(2)}) collective-permute-start(s32[27,512]{1,0:T(8,128)} %get-tuple-element.26), channel_id=1, source_target_pairs={{0,4},{4,8},{8,12},{12,16},{16,20},{20,24},{24,28},{1,5},{5,9},{9,... | collective-permute-start | bytes 165896 | tf_op jit(solution)/shard_map/ppermute | solution.py:391
  12.3 28.1 %copy-start.12 = (s32[1,512]{1,0:T(1,128)}, s32[1,512]{1,0:T(1,128)S(1)}, u32[]{:S(2)}) copy-start(s32[1,512]{1,0:T(1,128)S(1)} %get-tuple-element.15) | copy-start | bytes 6148
  13.8 19.9 %copy-start.10 = (s32[1,512]{1,0:T(1,128)}, s32[1,512]{1,0:T(1,128)S(1)}, u32[]{:S(2)}) copy-start(s32[1,512]{1,0:T(1,128)S(1)} %compare_select_fusion.4) | copy-start | bytes 6148
  24.1 1.6 copy-start.1
  25.6 1.1 copy-start.2
  26.8 1.1 copy-start.6
  31.0 1.4 copy-start.4
  32.4 1.3 copy-start.5
  34.8 12.3 %all-to-all-start = ((f32[8,2,512]{2,1,0:T(2,128)}), f32[8,2,512]{2,1,0:T(2,128)S(1)}, u32[]{:S(2)}, u32[]{:S(2)}) async-start(f32[8,2,512]{2,1,0:T(2,128)} %reshape.191), calls=%async_computation | async-start | bytes 65536 | tf_op jit(solution)/shard_map/all_to_all | solution.py:420
  42.7 13.9 %copy-start.9 = (s32[1,27,512]{2,0,1:T(1,128)S(1)}, s32[1,27,512]{2,0,1:T(1,128)}, u32[]{:S(2)}) copy-start(s32[1,27,512]{2,0,1:T(1,128)} %param.11) | copy-start | bytes 165892
  47.1 21.3 %copy-start.3 = (bf16[27,192,192]{2,1,0:T(8,128)(2,1)S(1)}, bf16[27,192,192]{2,1,0:T(8,128)(2,1)}, u32[]{:S(2)}) copy-start(bf16[27,192,192]{2,1,0:T(8,128)(2,1)} %weight.1) | copy-start | bytes 5971972
  47.2 4.0 %copy-start.14 = (s32[16]{0:T(128)}, s32[16]{0:T(128)S(1)}, u32[]{:S(2)}) copy-start(s32[16]{0:T(128)S(1)} %fusion.29) | copy-start | bytes 196
  50.0 11.1 %collective-permute-start.1 = (bf16[384,512]{1,0:T(8,128)(2,1)}, bf16[384,512]{1,0:T(8,128)(2,1)}, u32[]{:S(2)}, u32[]{:S(2)}) collective-permute-start(bf16[384,512]{1,0:T(8,128)(2,1)} %pad_maximum_fusion.1.own), channel_id=1, source_target_pairs={{4,0},{8,4},{12,8},{16,12},{20,16},{24,20},{28,24},{5,1},{9,5},{13... | collective-permute-start | bytes 1179656 | tf_op jit(solution)/shard_map/ppermute | solution.py:431
  51.3 17.1 %collective-permute-start = (bf16[384,512]{1,0:T(8,128)(2,1)}, bf16[384,512]{1,0:T(8,128)(2,1)}, u32[]{:S(2)}, u32[]{:S(2)}) collective-permute-start(bf16[384,512]{1,0:T(8,128)(2,1)} %pad_maximum_fusion.1.own), channel_id=1, source_target_pairs={{0,4},{4,8},{8,12},{12,16},{16,20},{20,24},{24,28},{1,5},{5,9},{9,... | collective-permute-start | bytes 1179656 | tf_op jit(solution)/shard_map/ppermute | solution.py:430
  59.5 51.6 %copy-start.15 = (s32[16]{0:T(128)S(1)}, s32[16]{0:T(128)}, u32[]{:S(2)}) copy-start(s32[16]{0:T(128)} %copy-done.14) | copy-start | bytes 196
  59.5 62.4 %copy-start.11 = (s32[1,512]{1,0:T(1,128)S(1)}, s32[1,512]{1,0:T(1,128)}, u32[]{:S(2)}) copy-start(s32[1,512]{1,0:T(1,128)} %copy-done.10) | copy-start | bytes 6148
  59.5 62.9 %copy-start.13 = (s32[1,512]{1,0:T(1,128)S(1)}, s32[1,512]{1,0:T(1,128)}, u32[]{:S(2)}) copy-start(s32[1,512]{1,0:T(1,128)} %copy-done.12) | copy-start | bytes 6148
  110.4 0.7 copy-start.7
  111.4 13.2 %copy-start.8 = (bf16[384,512]{1,0:T(8,128)(2,1)S(1)}, bf16[384,512]{1,0:T(8,128)(2,1)}, u32[]{:S(2)}) copy-start(bf16[384,512]{1,0:T(8,128)(2,1)} %copy-done.7) | copy-start | bytes 1179652
  133.6 2.0 copy-start

commit v4 on v3

--- a/solution.py
+++ b/solution.py
@@ -27,10 +27,11 @@
         acc_up[...] = jnp.zeros_like(acc_up)
         acc_down[...] = jnp.zeros_like(acc_down)
 
-    rows = lax.broadcasted_iota(jnp.int32, (count, count), 0)
+    rows = lax.broadcasted_iota(jnp.int32, (count, count), 0).astype(jnp.int16)
 
     def hot(ids):
-        return jnp.where(rows == ids, 1.0, 0.0).astype(jnp.bfloat16)
+        near = jnp.clip(ids, -1, count).astype(jnp.int16)
+        return jnp.where(rows == near, jnp.bfloat16(1), jnp.bfloat16(0))
 
     weight_here = weight[0]
     gathered = jnp.zeros((channels, count), jnp.float32)
@@ -97,7 +98,8 @@
 
 
 UNIT = 16
-PIECES = (5 * UNIT, 4 * UNIT)
+PIECES = (3 * UNIT, 2 * UNIT, 2 * UNIT, 2 * UNIT)
+STREAMS = range(len(PIECES))
 FAR = 4
 
 
@@ -137,7 +139,7 @@
         return pl.ds(pl.multiple_of(start, UNIT), size)
 
     def add(target, target_at, left, left_at, others, size):
-        chunk = 80 if size % 80 == 0 else 64
+        chunk = 48 if size % 48 == 0 else 32
 
         def body(i, carry):
             step = i * chunk
@@ -150,19 +152,19 @@
         lax.fori_loop(0, size // chunk, body, 0)
 
     half = 4 * FAR * sum(PIECES)
-    base = [0, 4 * FAR * PIECES[0]]
+    base = [4 * FAR * sum(PIECES[:s]) for s in STREAMS]
     whole = [4 * FAR * p for p in PIECES]
-    first_peer, second_peer = (y_peer, x_peer), (x_peer, y_peer)
-    first_bit, second_bit = (y, x), (x, y)
+    first_peer, second_peer = (y_peer, x_peer) * 2, (x_peer, y_peer) * 2
+    first_bit, second_bit = (y, x) * 2, (x, y) * 2
     mine, other = core * half, (1 - core) * half
     sent = []
 
     core_copies = [
         push(x_ref.at[at(other + base[s], whole[s])], got_core.at[at(base[s], whole[s])], core_peer)
-        for s in (0, 1)
+        for s in STREAMS
     ]
     ones = []
-    for s in (0, 1):
+    for s in STREAMS:
         core_copies[s].wait_recv()
         size = whole[s] // 2
         away = base[s] + (1 - first_bit[s]) * size
@@ -177,7 +179,7 @@
         stay = base[s] + first_bit[s] * size
         add(acc, stay, x_ref, mine + stay, [(got_core, stay)], size)
     twos = []
-    for s in (0, 1):
+    for s in STREAMS:
         ones[s].wait_recv()
         size = whole[s] // 4
         start = base[s] + first_bit[s] * (whole[s] // 2)
@@ -193,7 +195,7 @@
         stay = second_bit[s] * size
         add(acc, start + stay, acc, start + stay, [(got_one, base[s] // 2 + stay)], size)
     fars = []
-    for s in (0, 1):
+    for s in STREAMS:
         twos[s].wait_recv()
         size = whole[s] // 4
         start = base[s] + first_bit[s] * (whole[s] // 2) + second_bit[s] * size
@@ -204,13 +206,13 @@
             copies.append(
                 push(
                     acc.at[at(start + theirs * PIECES[s], PIECES[s])],
-                    got_far.at[at((k - 1) * sum(PIECES) + s * PIECES[0], PIECES[s])],
+                    got_far.at[at((k - 1) * sum(PIECES) + sum(PIECES[:s]), PIECES[s])],
                     far_peers[k - 1],
                 )
             )
         fars.append(copies)
     back = []
-    for s in (0, 1):
+    for s in STREAMS:
         for copy in fars[s]:
             copy.wait_recv()
         start = base[s] + first_bit[s] * (whole[s] // 2) + second_bit[s] * (whole[s] // 4)
@@ -220,13 +222,13 @@
             mine + piece,
             acc,
             piece,
-            [(got_far, k * sum(PIECES) + s * PIECES[0]) for k in range(FAR - 1)],
+            [(got_far, k * sum(PIECES) + sum(PIECES[:s])) for k in range(FAR - 1)],
             PIECES[s],
         )
         span = at(mine + piece, PIECES[s])
         back.append([push(out_ref.at[span], out_ref.at[span], peer) for peer in far_peers])
     two_back = []
-    for s in (0, 1):
+    for s in STREAMS:
         for copy in back[s]:
             copy.wait_recv()
         size = whole[s] // 4
@@ -234,28 +236,28 @@
         span = at(mine + start, size)
         two_back.append(push(out_ref.at[span], out_ref.at[span], second_peer[s]))
     one_back = []
-    for s in (0, 1):
+    for s in STREAMS:
         two_back[s].wait_recv()
         size = whole[s] // 2
         span = at(mine + base[s] + first_bit[s] * size, size)
         one_back.append(push(out_ref.at[span], out_ref.at[span], first_peer[s]))
     core_back = []
-    for s in (0, 1):
+    for s in STREAMS:
         one_back[s].wait_recv()
         span = at(mine + base[s], whole[s])
         core_back.append(push(out_ref.at[span], out_ref.at[span], core_peer))
     for copy in core_back:
         copy.wait_recv()
-    for copy in core_copies + ones + twos + fars[0] + fars[1]:
+    for copy in core_copies + ones + twos + sum(fars + back, []):
         copy.wait_send()
-    for copy in back[0] + back[1] + two_back + one_back + core_back:
+    for copy in two_back + one_back + core_back:
         copy.wait_send()
 
 
 def reduce_call(partial):
     rows, columns = partial.shape
     assert rows == 8 * FAR * sum(PIECES)
-    copies = 6 + 2 * (FAR - 1) + 6 + 2 * (FAR - 1)
+    copies = len(PIECES) * 2 * (3 + FAR - 1)
     kind = partial.dtype
     return pl.pallas_call(
         reduce_kernel,

time: 203 us -> 195 us (0.961)
  Pallas kernels: 113 us -> 106 us
    pallas_call x1, Pallas kernels: 60.4 us -> 53.2 us  [reduce_call(): pl.pallas_call(reduce_kernel, in_specs=[pl.BlockSpec(memory_space=pltpu.V...]
where the time goes in v4:
time: 195 us; the launch traced here: 194 us
  Pallas kernels  106 us (54%)
  local copies, waits for them, and re-layouts  28.6 us (15%)
  starting transfers between devices  19.6 us (10%)
  waiting for transfers between devices  13.1 us (7%)
  blocking collectives  10.5 us (5%)
  other arithmetic  8.19 us (4%)
  matrix products  7.61 us (4%)
    pallas_call x1, Pallas kernels, reduce_call(): pl.pallas_call(reduce_kernel, in_specs=[pl.BlockSpec(memory_space=pltpu.V...  53.2 us
    pallas_call x1, Pallas kernels, conv_call(): pl.pallas_call(conv_kernel, grid=(offsets,), in_specs=[pl.BlockSpec((2 *...  41.6 us
    unnamed x35, local copies, waits for them, and re-layouts  18.5 us
    all_to_all x1, blocking collectives, per_device(): lax.all_to_all(outgoing.reshape(vox_count, CAP, 2 * channels), 'vox', spl...  10.5 us
    pallas_call x1, Pallas kernels, outer_call(): pl.pallas_call(functools.partial(outer_kernel, kids), grid=(blocks - take...  7.91 us
    dot_general x8, matrix products, dot(): lax.dot_general(left, right, (dims, ((), ())), precision=precision, prefe...  7.61 us
    ppermute x1, waiting for transfers between devices, per_device(): before = lax.ppermute(own, 'vox', up)  7.32 us
    ppermute x1, starting transfers between devices, per_device(): lax.ppermute(near_next, 'vox', up)  6.11 us
  transfers between devices with their start and end apart: 5, of which 3 were waited for; matrix products, arithmetic and copies ran while one was open for 12% of the time, Pallas kernels for 2%

profile of v4, /device:TPU:0, one launch (start us, length us, event | category | flops | bytes accessed | tf_op | source)
XLA Modules:
  0.0 194.3 jit_solution(5705442685439853291)
XLA Ops:
  0.6 1.5 fusion.12
  2.1 1.3 collective-permute-start.3
  3.4 6.1 %collective-permute-start.2 = (s32[27,512]{1,0:T(8,128)}, s32[27,512]{1,0:T(8,128)}, u32[]{:S(2)}, u32[]{:S(2)}) collective-permute-start(s32[27,512]{1,0:T(8,128)} %get-tuple-element.26), channel_id=1, source_target_pairs={{0,4},{4,8},{8,12},{12,16},{16,20},{20,24},{24,28},{1,5},{5,9},{9,... | collective-permute-start | bytes 165896 | tf_op jit(solution)/shard_map/ppermute | solution.py:393
  9.5 0.7 broadcast_add_fusion
  10.2 0.7 broadcast_compare_fusion.1
  10.9 0.7 broadcast_compare_fusion
  11.6 0.7 compare_select_fusion.5
  12.3 1.1 reduce-window.6
  13.5 0.2 slice_reduce_fusion
  13.7 0.1 fusion.19
  13.8 0.1 select_reduce_fusion
  14.0 0.8 convert_reduce_fusion
  14.7 0.2 convert_element_type.42.occupied
  14.9 2.2 %copy.70 = bf16[192,8,192]{2,0,1:T(8,128)(2,1)} copy(bf16[192,8,192]{2,1,0:T(8,128)(2,1)} %param.15) | data formatting | bytes 1179648 | tf_op args[7]
  17.1 3.1 %copy.53 = bf16[1,4096,192]{2,1,0:T(8,128)(2,1)S(1)} copy(bf16[1,4096,192]{1,2,0:T(8,128)(2,1)} %param.8) | data formatting | bytes 3145728 | tf_op args[0]
  20.2 3.8 %copy.54 = bf16[1,4096,192]{2,1,0:T(8,128)(2,1)} copy(bf16[1,4096,192]{1,2,0:T(8,128)(2,1)} %param.12) | data formatting | bytes 3145728 | tf_op args[4]
  24.1 1.6 copy-done.1
  25.6 1.1 copy-done.2
  26.8 1.1 copy-done.6
  27.9 3.1 %shard_map.103 = (bf16[8,512,192]{2,1,0:T(8,128)(2,1)S(1)}, bf16[8,512,192]{2,1,0:T(8,128)(2,1)S(1)}, f32[512,384]{1,0:T(8,128)S(1)}) custom-call(bf16[4096,192]{1,0:T(8,128)(2,1)S(1)} %bitcast.38, bf16[4096,192]{1,0:T(8,128)(2,1)S(1)} %bitcast.39, f32[512,8]{1,0:T(8,128)S(1)} %convert_element_type.42.occupied, bf16[8,192,192]{2,1,0:T(8,128)(2,1)S(1)} %copy-done.6, ...), custom_call_target="tpu_custom_call" | custom-call | tf_op jit(solution)/shard_map/pallas_call | solution.py:314
  31.0 0.0 copy-start.4
  31.0 1.3 copy-done.4
  32.4 1.3 copy-done.5
  33.7 0.4 fusion.17
  34.1 0.1 broadcast_in_dim.45
  34.1 0.6 reshape.191
  34.8 5.6 %all-to-all-start = ((f32[8,2,512]{2,1,0:T(2,128)}), f32[8,2,512]{2,1,0:T(2,128)S(1)}, u32[]{:S(2)}, u32[]{:S(2)}) async-start(f32[8,2,512]{2,1,0:T(2,128)} %reshape.191), calls=%async_computation | async-start | bytes 65536 | tf_op jit(solution)/shard_map/all_to_all | solution.py:422
  40.4 2.3 %fusion.1 = f32[384,512]{1,0:T(8,128)} fusion(f32[512,384]{1,0:T(8,128)S(1)} %get-tuple-element.8, s32[512]{0:T(512)S(1)} %bitcast.52), kind=kOutput, calls=%fused_computation.9 | convolution fusion | flops 1208221696 | bytes 1574912 | tf_op jit(solution)/shard_map/dot_general | solution.py:14
  42.7 4.3 %all-to-all-done = f32[8,2,512]{2,1,0:T(2,128)S(1)} async-done(((f32[8,2,512]{2,1,0:T(2,128)}), f32[8,2,512]{2,1,0:T(2,128)S(1)}, u32[]{:S(2)}, u32[]{:S(2)}) %all-to-all-start) | async-done | bytes 32800 | tf_op jit(solution)/shard_map/all_to_all | solution.py:422
  47.1 0.0 copy-start.3
  47.1 0.1 fusion.29
  47.2 1.8 convolution_add_fusion.wide
  49.1 0.1 multiply_convert_fusion
  49.2 0.8 pad_maximum_fusion.1.own
  50.0 1.3 collective-permute-start.1
  51.3 5.3 %collective-permute-start = (bf16[384,512]{1,0:T(8,128)(2,1)}, bf16[384,512]{1,0:T(8,128)(2,1)}, u32[]{:S(2)}, u32[]{:S(2)}) collective-permute-start(bf16[384,512]{1,0:T(8,128)(2,1)} %pad_maximum_fusion.1.own), channel_id=1, source_target_pairs={{0,4},{4,8},{8,12},{12,16},{16,20},{20,24},{24,28},{1,5},{5,9},{9,... | collective-permute-start | bytes 1179656 | tf_op jit(solution)/shard_map/ppermute | solution.py:432
  56.6 0.1 fusion.14.ids_out
  56.6 0.9 copy.58
  57.5 0.0 collective-permute-done.2
  57.6 0.9 copy.57
  58.5 0.0 collective-permute-done.3
  58.5 0.9 concatenate.27
  59.4 0.2 fusion.8.ids_in
  59.5 1.5 collective-permute-done.1.after
  61.0 7.3 %collective-permute-done.before = bf16[384,512]{1,0:T(8,128)(2,1)} collective-permute-done((bf16[384,512]{1,0:T(8,128)(2,1)}, bf16[384,512]{1,0:T(8,128)(2,1)}, u32[]{:S(2)}, u32[]{:S(2)}) %collective-permute-start) | collective-permute-done | bytes 393248 | tf_op jit(solution)/shard_map/ppermute | solution.py:432
  68.4 41.6 %shard_map.104 = (bf16[4608,384]{1,0:T(8,128)(2,1)}, bf16[384,512]{1,0:T(8,128)(2,1)S(1)}) custom-call(bf16[384,512]{1,0:T(8,128)(2,1)} %collective-permute-done.before, bf16[384,512]{1,0:T(8,128)(2,1)} %pad_maximum_fusion.1.own, bf16[384,512]{1,0:T(8,128)(2,1)} %collective-permute-done.1.after, f32[384,512]{1,0:T(8,128)S(1)} %convolution_add_fusion.wide, ...), custom_call_target="tpu_custom_call" | custom-call | tf_op jit(solution)/shard_map/pallas_call | solution.py:76
  109.9 0.7 copy-done.7
  110.7 0.2 convolution_convert_fusion
  111.0 10.5 %all_to_all.10 = bf16[8,2,384]{2,1,0:T(2,128)(2,1)S(1)} all-to-all(bf16[8,2,384]{2,1,0:T(2,128)(2,1)S(1)} %reshape.193), channel_id=1, replica_groups=mesh['vox'=8,'rep'=4] {'vox'}, dimensions={0} | all-to-all | bytes 24576 | tf_op jit(solution)/shard_map/all_to_all | solution.py:440
  121.5 0.3 fusion.15
  121.8 0.2 fusion.16
  122.0 1.3 convolution_add_fusion.1
  123.3 0.8 copy.59.down_rows
  124.2 1.0 fusion.up_rows
  125.2 7.9 %shard_map.105.x_ref = bf16[4608,384]{1,0:T(8,128)(2,1)} custom-call(bf16[192,512]{1,0:T(8,128)(2,1)} %fusion.up_rows, bf16[512,192]{1,0:T(8,128)(2,1)} %copy.59.down_rows, bf16[8,512,192]{2,1,0:T(8,128)(2,1)} %copy-done.5, bf16[8,512,192]{2,1,0:T(8,128)(2,1)} %copy-done.4, bf16[4608,384]{1,0:T(8,128)(2,1)} %get-tuple-element.12.packed), custom_call_target="tpu_custom_call", output_to_operand_aliasing={{}: (4, {})} | custom-call | tf_op jit(solution)/shard_map/pallas_call | solution.py:348
  133.1 2.0 %copy-done = bf16[4608,384]{1,0:T(8,128)(2,1)S(1)} copy-done((bf16[4608,384]{1,0:T(8,128)(2,1)S(1)}, bf16[4608,384]{1,0:T(8,128)(2,1)}, u32[]{:S(2)}) %copy-start) | copy-done | bytes 3538968
  135.1 53.2 %shard_map.106 = bf16[4608,384]{1,0:T(8,128)(2,1)S(1)} custom-call(bf16[4608,384]{1,0:T(8,128)(2,1)S(1)} %copy-done), custom_call_target="tpu_custom_call" | custom-call | tf_op jit(solution)/shard_map/pallas_call | solution.py:262
  188.3 1.2 fusion.34
  189.5 0.2 slice.63
  189.7 1.3 copy.69
  191.1 0.7 slice_bitcast_fusion.1
  191.7 0.5 pad_maximum_fusion
  192.3 0.3 copy.60
  192.6 1.7 slice.77
  (33 shorter events, 0.2 us)
Async XLA Ops:
  2.1 56.4 %collective-permute-start.3 = (s32[27,512]{1,0:T(8,128)}, s32[27,512]{1,0:T(8,128)}, u32[]{:S(2)}, u32[]{:S(2)}) collective-permute-start(s32[27,512]{1,0:T(8,128)} %get-tuple-element.26), channel_id=1, source_target_pairs={{4,0},{8,4},{12,8},{16,12},{20,16},{24,20},{28,24},{5,1},{9,5},{13... | collective-permute-start | bytes 165896 | tf_op jit(solution)/shard_map/ppermute | solution.py:393
  3.4 54.2 %collective-permute-start.2 = (s32[27,512]{1,0:T(8,128)}, s32[27,512]{1,0:T(8,128)}, u32[]{:S(2)}, u32[]{:S(2)}) collective-permute-start(s32[27,512]{1,0:T(8,128)} %get-tuple-element.26), channel_id=1, source_target_pairs={{0,4},{4,8},{8,12},{12,16},{16,20},{20,24},{24,28},{1,5},{5,9},{9,... | collective-permute-start | bytes 165896 | tf_op jit(solution)/shard_map/ppermute | solution.py:393
  12.3 28.1 %copy-start.12 = (s32[1,512]{1,0:T(1,128)}, s32[1,512]{1,0:T(1,128)S(1)}, u32[]{:S(2)}) copy-start(s32[1,512]{1,0:T(1,128)S(1)} %get-tuple-element.15) | copy-start | bytes 6148
  13.8 19.9 %copy-start.10 = (s32[1,512]{1,0:T(1,128)}, s32[1,512]{1,0:T(1,128)S(1)}, u32[]{:S(2)}) copy-start(s32[1,512]{1,0:T(1,128)S(1)} %compare_select_fusion.4) | copy-start | bytes 6148
  24.1 1.6 copy-start.1
  25.6 1.1 copy-start.2
  26.8 1.1 copy-start.6
  31.0 1.4 copy-start.4
  32.4 1.3 copy-start.5
  34.8 12.3 %all-to-all-start = ((f32[8,2,512]{2,1,0:T(2,128)}), f32[8,2,512]{2,1,0:T(2,128)S(1)}, u32[]{:S(2)}, u32[]{:S(2)}) async-start(f32[8,2,512]{2,1,0:T(2,128)} %reshape.191), calls=%async_computation | async-start | bytes 65536 | tf_op jit(solution)/shard_map/all_to_all | solution.py:422
  42.7 13.9 %copy-start.9 = (s32[1,27,512]{2,0,1:T(1,128)S(1)}, s32[1,27,512]{2,0,1:T(1,128)}, u32[]{:S(2)}) copy-start(s32[1,27,512]{2,0,1:T(1,128)} %param.11) | copy-start | bytes 165892
  47.1 21.3 %copy-start.3 = (bf16[27,192,192]{2,1,0:T(8,128)(2,1)S(1)}, bf16[27,192,192]{2,1,0:T(8,128)(2,1)}, u32[]{:S(2)}) copy-start(bf16[27,192,192]{2,1,0:T(8,128)(2,1)} %weight.1) | copy-start | bytes 5971972
  47.2 4.0 %copy-start.14 = (s32[16]{0:T(128)}, s32[16]{0:T(128)S(1)}, u32[]{:S(2)}) copy-start(s32[16]{0:T(128)S(1)} %fusion.29) | copy-start | bytes 196
  50.0 11.1 %collective-permute-start.1 = (bf16[384,512]{1,0:T(8,128)(2,1)}, bf16[384,512]{1,0:T(8,128)(2,1)}, u32[]{:S(2)}, u32[]{:S(2)}) collective-permute-start(bf16[384,512]{1,0:T(8,128)(2,1)} %pad_maximum_fusion.1.own), channel_id=1, source_target_pairs={{4,0},{8,4},{12,8},{16,12},{20,16},{24,20},{28,24},{5,1},{9,5},{13... | collective-permute-start | bytes 1179656 | tf_op jit(solution)/shard_map/ppermute | solution.py:433
  51.3 17.1 %collective-permute-start = (bf16[384,512]{1,0:T(8,128)(2,1)}, bf16[384,512]{1,0:T(8,128)(2,1)}, u32[]{:S(2)}, u32[]{:S(2)}) collective-permute-start(bf16[384,512]{1,0:T(8,128)(2,1)} %pad_maximum_fusion.1.own), channel_id=1, source_target_pairs={{0,4},{4,8},{8,12},{12,16},{16,20},{20,24},{24,28},{1,5},{5,9},{9,... | collective-permute-start | bytes 1179656 | tf_op jit(solution)/shard_map/ppermute | solution.py:432
  59.5 51.2 %copy-start.15 = (s32[16]{0:T(128)S(1)}, s32[16]{0:T(128)}, u32[]{:S(2)}) copy-start(s32[16]{0:T(128)} %copy-done.14) | copy-start | bytes 196
  59.5 61.9 %copy-start.11 = (s32[1,512]{1,0:T(1,128)S(1)}, s32[1,512]{1,0:T(1,128)}, u32[]{:S(2)}) copy-start(s32[1,512]{1,0:T(1,128)} %copy-done.10) | copy-start | bytes 6148
  59.5 62.5 %copy-start.13 = (s32[1,512]{1,0:T(1,128)S(1)}, s32[1,512]{1,0:T(1,128)}, u32[]{:S(2)}) copy-start(s32[1,512]{1,0:T(1,128)} %copy-done.12) | copy-start | bytes 6148
  109.9 0.7 copy-start.7
  110.9 13.2 %copy-start.8 = (bf16[384,512]{1,0:T(8,128)(2,1)S(1)}, bf16[384,512]{1,0:T(8,128)(2,1)}, u32[]{:S(2)}) copy-start(bf16[384,512]{1,0:T(8,128)(2,1)} %copy-done.7) | copy-start | bytes 1179652
  133.1 2.0 %copy-start = (bf16[4608,384]{1,0:T(8,128)(2,1)S(1)}, bf16[4608,384]{1,0:T(8,128)(2,1)}, u32[]{:S(2)}) copy-start(bf16[4608,384]{1,0:T(8,128)(2,1)} %shard_map.105.x_ref) | copy-start | bytes 10616836

commit v5 on v4

--- a/solution.py
+++ b/solution.py
@@ -17,7 +17,7 @@
 
 
 def conv_kernel(
-    before, own, after, wide, ids_out, ids_in, weight, term_ref, both_ref, acc_up, acc_down
+    before, own, after, wide, ids_out, ids_in, weight_even, weight_odd, term_ref, both_ref, acc_up, acc_down
 ):
     step = pl.program_id(0)
     channels, count = acc_up.shape
@@ -33,28 +33,24 @@
         near = jnp.clip(ids, -1, count).astype(jnp.int16)
         return jnp.where(rows == near, jnp.bfloat16(1), jnp.bfloat16(0))
 
-    weight_here = weight[0]
-    gathered = jnp.zeros((channels, count), jnp.float32)
+    up_part = jnp.zeros((channels, count), jnp.float32)
     spread = acc_down[...]
-    for at, block in enumerate((before, own, after)):
-        gathered += dot(
-            block[:channels, :], hot(ids_out[0] - at * count), ((1,), (0,))
-        )
-        moved = dot(weight_here, block[channels:, :], ((1,), (0,))).astype(jnp.bfloat16)
-        spread += dot(moved, hot(ids_in[0, :, at * count : (at + 1) * count]), ((1,), (1,)))
+    for part, weight in enumerate((weight_even, weight_odd)):
+        weight_here = weight[0]
+        gathered = jnp.zeros((channels, count), jnp.float32)
+        for at, block in enumerate((before, own, after)):
+            gathered += dot(
+                block[:channels, :], hot(ids_out[part] - at * count), ((1,), (0,))
+            )
+            moved = dot(weight_here, block[channels:, :], ((1,), (0,))).astype(jnp.bfloat16)
+            near = ids_in[part, :, at * count : (at + 1) * count]
+            spread += dot(moved, hot(near), ((1,), (1,)))
+        gathered = gathered.astype(jnp.bfloat16)
+        up_part += dot(weight_here, gathered, ((0,), (0,)))
+        term = dot(gathered, own[channels:, :], ((1,), (1,)))
+        term_ref[:, part * channels : (part + 1) * channels] = term.astype(term_ref.dtype)
     acc_down[...] = spread
-    gathered = gathered.astype(jnp.bfloat16)
-    acc_up[...] += dot(weight_here, gathered, ((0,), (0,)))
-    term = dot(gathered, own[channels:, :], ((1,), (1,))).astype(term_ref.dtype)
-
-    @pl.when(step % 2 == 0)
-    def _():
-        term_ref[:, :channels] = term
-        term_ref[:, channels:] = jnp.zeros_like(term)
-
-    @pl.when(step % 2 == 1)
-    def _():
-        term_ref[:, channels:] = term
+    acc_up[...] += up_part
 
     @pl.when(step == pl.num_programs(0) - 1)
     def _():
@@ -72,18 +68,22 @@
     offsets, channels = conv_weight.shape[:2]
     count = own.shape[1]
     whole = lambda j: (0, 0)
+    padded = lambda ids: jnp.pad(ids, ((0, offsets % 2), (0, 0), (0, 0)), constant_values=-1)
     each = lambda j: (j, 0, 0)
     return pl.pallas_call(
         conv_kernel,
-        grid=(offsets,),
+        grid=((offsets + 1) // 2,),
         in_specs=[pl.BlockSpec((2 * channels, count), whole)] * 4
         + [
-            pl.BlockSpec((1, 1, count), each),
-            pl.BlockSpec((1, 1, 3 * count), each),
-            pl.BlockSpec((1, channels, channels), each),
+            pl.BlockSpec((2, 1, count), each),
+            pl.BlockSpec((2, 1, 3 * count), each),
+            pl.BlockSpec((1, channels, channels), lambda j: (2 * j, 0, 0)),
+            pl.BlockSpec(
+                (1, channels, channels), lambda j: (jnp.minimum(2 * j + 1, offsets - 1), 0, 0)
+            ),
         ],
         out_specs=[
-            pl.BlockSpec((channels, 2 * channels), lambda j: (j // 2, 0)),
+            pl.BlockSpec((channels, 2 * channels), lambda j: (j, 0)),
             pl.BlockSpec((2 * channels, count), whole),
         ],
         out_shape=[
@@ -94,7 +94,7 @@
         ],
         scratch_shapes=[pltpu.VMEM((channels, count), jnp.float32)] * 2,
         compiler_params=pltpu.CompilerParams(vmem_limit_bytes=48 * 1024 * 1024),
-    )(before, own, after, wide, ids_out, ids_in, conv_weight)
+    )(before, own, after, wide, padded(ids_out), padded(ids_in), conv_weight, conv_weight)
 
 
 UNIT = 16

time: 195 us -> 193 us (0.990)
  Pallas kernels: 106 us -> 103 us
    pallas_call x1, Pallas kernels: 41.6 us -> 39.4 us  [conv_call(): pl.pallas_call(conv_kernel, grid=((offsets + 1) // 2,), in_specs=[pl.Bloc...]
    unnamed x35 -> x21, local copies, waits for them, and re-layouts: 18.5 us -> 18.4 us
  transfers between devices with their start and end apart: 5 -> 5, of which waited for: 3 -> 2; matrix products, arithmetic and copies ran while one was open for 12% -> 13% of each run, Pallas kernels for 2% -> 2%
where the time goes in v5:
time: 193 us; the launch traced here: 192 us
  Pallas kernels  103 us (53%)
  local copies, waits for them, and re-layouts  28.7 us (15%)
  starting transfers between devices  19.6 us (10%)
  waiting for transfers between devices  11.6 us (6%)
  blocking collectives  10.5 us (5%)
  other arithmetic  9.6 us (5%)
  matrix products  7.61 us (4%)
    pallas_call x1, Pallas kernels, reduce_call(): pl.pallas_call(reduce_kernel, in_specs=[pl.BlockSpec(memory_space=pltpu.V...  53 us
    pallas_call x1, Pallas kernels, conv_call(): pl.pallas_call(conv_kernel, grid=((offsets + 1) // 2,), in_specs=[pl.Bloc...  39.4 us
    unnamed x21, local copies, waits for them, and re-layouts  18.4 us
    all_to_all x1, blocking collectives, per_device(): lax.all_to_all(outgoing.reshape(vox_count, CAP, 2 * channels), 'vox', spl...  10.5 us
    pallas_call x1, Pallas kernels, outer_call(): pl.pallas_call(functools.partial(outer_kernel, kids), grid=(blocks - take...  7.97 us
    dot_general x8, matrix products, dot(): lax.dot_general(left, right, (dims, ((), ())), precision=precision, prefe...  7.61 us
    ppermute x1, waiting for transfers between devices, per_device(): before = lax.ppermute(own, 'vox', up)  7.26 us
    ppermute x1, starting transfers between devices, per_device(): lax.ppermute(near_next, 'vox', up)  6.1 us
  transfers between devices with their start and end apart: 5, of which 2 were waited for; matrix products, arithmetic and copies ran while one was open for 13% of the time, Pallas kernels for 2%

profile of v5, /device:TPU:0, one launch (start us, length us, event | category | flops | bytes accessed | tf_op | source)
XLA Modules:
  0.0 191.9 jit_solution(17146248689401432462)
XLA Ops:
  0.6 1.5 fusion.12
  2.1 1.3 collective-permute-start.3
  3.4 6.1 %collective-permute-start.2 = (s32[27,512]{1,0:T(8,128)}, s32[27,512]{1,0:T(8,128)}, u32[]{:S(2)}, u32[]{:S(2)}) collective-permute-start(s32[27,512]{1,0:T(8,128)} %get-tuple-element.26), channel_id=1, source_target_pairs={{0,4},{4,8},{8,12},{12,16},{16,20},{20,24},{24,28},{1,5},{5,9},{9,... | collective-permute-start | bytes 165896 | tf_op jit(solution)/shard_map/ppermute | solution.py:393
  9.5 0.7 broadcast_add_fusion
  10.2 0.7 broadcast_compare_fusion.1
  10.9 0.7 broadcast_compare_fusion
  11.6 0.7 compare_select_fusion.5
  12.3 1.1 reduce-window.6
  13.4 0.2 slice_reduce_fusion
  13.7 0.1 fusion.19
  13.8 0.1 select_reduce_fusion
  13.9 0.8 convert_reduce_fusion
  14.7 0.2 convert_element_type.42.occupied
  14.8 2.2 %copy.70 = bf16[192,8,192]{2,0,1:T(8,128)(2,1)} copy(bf16[192,8,192]{2,1,0:T(8,128)(2,1)} %param.15) | data formatting | bytes 1179648 | tf_op args[7]
  17.0 3.1 %copy.53 = bf16[1,4096,192]{2,1,0:T(8,128)(2,1)S(1)} copy(bf16[1,4096,192]{1,2,0:T(8,128)(2,1)} %param.8) | data formatting | bytes 3145728 | tf_op args[0]
  20.2 3.8 %copy.54 = bf16[1,4096,192]{2,1,0:T(8,128)(2,1)} copy(bf16[1,4096,192]{1,2,0:T(8,128)(2,1)} %param.12) | data formatting | bytes 3145728 | tf_op args[4]
  24.0 1.6 copy-done.2
  25.6 1.1 copy-done.3
  26.7 1.1 copy-done.6
  27.9 3.1 %shard_map.103 = (bf16[8,512,192]{2,1,0:T(8,128)(2,1)S(1)}, bf16[8,512,192]{2,1,0:T(8,128)(2,1)S(1)}, f32[512,384]{1,0:T(8,128)S(1)}) custom-call(bf16[4096,192]{1,0:T(8,128)(2,1)S(1)} %bitcast.38, bf16[4096,192]{1,0:T(8,128)(2,1)S(1)} %bitcast.39, f32[512,8]{1,0:T(8,128)S(1)} %convert_element_type.42.occupied, bf16[8,192,192]{2,1,0:T(8,128)(2,1)S(1)} %copy-done.6, ...), custom_call_target="tpu_custom_call" | custom-call | tf_op jit(solution)/shard_map/pallas_call | solution.py:314
  31.0 1.4 copy-done.4
  32.3 1.3 copy-done.5
  33.7 0.4 fusion.17
  34.0 0.1 broadcast_in_dim.45
  34.1 0.6 reshape.191
  34.7 5.6 %all-to-all-start = ((f32[8,2,512]{2,1,0:T(2,128)}), f32[8,2,512]{2,1,0:T(2,128)S(1)}, u32[]{:S(2)}, u32[]{:S(2)}) async-start(f32[8,2,512]{2,1,0:T(2,128)} %reshape.191), calls=%async_computation | async-start | bytes 65536 | tf_op jit(solution)/shard_map/all_to_all | solution.py:422
  40.4 2.3 %fusion.1 = f32[384,512]{1,0:T(8,128)} fusion(f32[512,384]{1,0:T(8,128)S(1)} %get-tuple-element.8, s32[512]{0:T(512)S(1)} %bitcast.52), kind=kOutput, calls=%fused_computation.9 | convolution fusion | flops 1208221696 | bytes 1574912 | tf_op jit(solution)/shard_map/dot_general | solution.py:14
  42.7 4.3 %all-to-all-done = f32[8,2,512]{2,1,0:T(2,128)S(1)} async-done(((f32[8,2,512]{2,1,0:T(2,128)}), f32[8,2,512]{2,1,0:T(2,128)S(1)}, u32[]{:S(2)}, u32[]{:S(2)}) %all-to-all-start) | async-done | bytes 32800 | tf_op jit(solution)/shard_map/all_to_all | solution.py:422
  47.1 0.1 fusion.29
  47.2 1.8 convolution_add_fusion.wide
  49.0 0.1 multiply_convert_fusion
  49.2 0.8 pad_maximum_fusion.1.own
  49.9 1.3 collective-permute-start.1
  51.2 5.3 %collective-permute-start = (bf16[384,512]{1,0:T(8,128)(2,1)}, bf16[384,512]{1,0:T(8,128)(2,1)}, u32[]{:S(2)}, u32[]{:S(2)}) collective-permute-start(bf16[384,512]{1,0:T(8,128)(2,1)} %pad_maximum_fusion.1.own), channel_id=1, source_target_pairs={{0,4},{4,8},{8,12},{12,16},{16,20},{20,24},{24,28},{1,5},{5,9},{9,... | collective-permute-start | bytes 1179656 | tf_op jit(solution)/shard_map/ppermute | solution.py:432
  56.5 1.5 fusion.14
  58.0 0.9 pad.8.ids_out
  58.9 0.1 copy.58
  59.0 0.0 collective-permute-done.2
  59.0 0.9 copy.57
  59.9 0.0 collective-permute-done.3
  59.9 0.9 concatenate.27
  60.8 0.2 fusion.8
  60.9 0.1 pad.9.ids_in
  61.1 0.0 collective-permute-done.1.after
  61.1 7.3 %collective-permute-done.before = bf16[384,512]{1,0:T(8,128)(2,1)} collective-permute-done((bf16[384,512]{1,0:T(8,128)(2,1)}, bf16[384,512]{1,0:T(8,128)(2,1)}, u32[]{:S(2)}, u32[]{:S(2)}) %collective-permute-start) | collective-permute-done | bytes 393248 | tf_op jit(solution)/shard_map/ppermute | solution.py:432
  68.3 39.4 %shard_map.104 = (bf16[4608,384]{1,0:T(8,128)(2,1)}, bf16[384,512]{1,0:T(8,128)(2,1)S(1)}) custom-call(bf16[384,512]{1,0:T(8,128)(2,1)} %collective-permute-done.before, bf16[384,512]{1,0:T(8,128)(2,1)} %pad_maximum_fusion.1.own, bf16[384,512]{1,0:T(8,128)(2,1)} %collective-permute-done.1.after, f32[384,512]{1,0:T(8,128)S(1)} %convolution_add_fusion.wide, ...), custom_call_target="tpu_custom_call" | custom-call | tf_op jit(solution)/shard_map/pallas_call | solution.py:73
  107.8 0.7 copy-done.7
  108.5 0.2 convolution_convert_fusion
  108.8 10.5 %all_to_all.10 = bf16[8,2,384]{2,1,0:T(2,128)(2,1)S(1)} all-to-all(bf16[8,2,384]{2,1,0:T(2,128)(2,1)S(1)} %reshape.193), channel_id=1, replica_groups=mesh['vox'=8,'rep'=4] {'vox'}, dimensions={0} | all-to-all | bytes 24576 | tf_op jit(solution)/shard_map/all_to_all | solution.py:440
  119.3 0.3 fusion.15
  119.6 0.2 fusion.16
  119.8 1.3 convolution_add_fusion.1
  121.1 0.8 copy.59.down_rows
  121.9 1.0 fusion.up_rows
  123.0 8.0 %shard_map.105.x_ref = bf16[4608,384]{1,0:T(8,128)(2,1)} custom-call(bf16[192,512]{1,0:T(8,128)(2,1)} %fusion.up_rows, bf16[512,192]{1,0:T(8,128)(2,1)} %copy.59.down_rows, bf16[8,512,192]{2,1,0:T(8,128)(2,1)} %copy-done.5, bf16[8,512,192]{2,1,0:T(8,128)(2,1)} %copy-done.4, bf16[4608,384]{1,0:T(8,128)(2,1)} %get-tuple-element.12.packed), custom_call_target="tpu_custom_call", output_to_operand_aliasing={{}: (4, {})} | custom-call | tf_op jit(solution)/shard_map/pallas_call | solution.py:348
  131.0 2.0 %copy-done = bf16[4608,384]{1,0:T(8,128)(2,1)S(1)} copy-done((bf16[4608,384]{1,0:T(8,128)(2,1)S(1)}, bf16[4608,384]{1,0:T(8,128)(2,1)}, u32[]{:S(2)}) %copy-start) | copy-done | bytes 3538968
  133.0 53.0 %shard_map.106 = bf16[4608,384]{1,0:T(8,128)(2,1)S(1)} custom-call(bf16[4608,384]{1,0:T(8,128)(2,1)S(1)} %copy-done), custom_call_target="tpu_custom_call" | custom-call | tf_op jit(solution)/shard_map/pallas_call | solution.py:262
  186.0 1.2 fusion.34
  187.2 0.2 slice.63
  187.4 1.3 copy.69
  188.7 0.7 slice_bitcast_fusion.1
  189.4 0.5 pad_maximum_fusion
  190.0 0.3 copy.60
  190.2 1.7 slice.77
  (21 shorter events, 0.2 us)
Async XLA Ops:
  2.1 57.8 %collective-permute-start.3 = (s32[27,512]{1,0:T(8,128)}, s32[27,512]{1,0:T(8,128)}, u32[]{:S(2)}, u32[]{:S(2)}) collective-permute-start(s32[27,512]{1,0:T(8,128)} %get-tuple-element.26), channel_id=1, source_target_pairs={{4,0},{8,4},{12,8},{16,12},{20,16},{24,20},{28,24},{5,1},{9,5},{13... | collective-permute-start | bytes 165896 | tf_op jit(solution)/shard_map/ppermute | solution.py:393
  3.4 55.6 %collective-permute-start.2 = (s32[27,512]{1,0:T(8,128)}, s32[27,512]{1,0:T(8,128)}, u32[]{:S(2)}, u32[]{:S(2)}) collective-permute-start(s32[27,512]{1,0:T(8,128)} %get-tuple-element.26), channel_id=1, source_target_pairs={{0,4},{4,8},{8,12},{12,16},{16,20},{20,24},{24,28},{1,5},{5,9},{9,... | collective-permute-start | bytes 165896 | tf_op jit(solution)/shard_map/ppermute | solution.py:393
  24.0 1.6 copy-start.2
  25.6 1.1 copy-start.3
  26.7 1.1 copy-start.6
  31.0 1.4 copy-start.4
  32.3 1.3 copy-start.5
  34.7 12.3 %all-to-all-start = ((f32[8,2,512]{2,1,0:T(2,128)}), f32[8,2,512]{2,1,0:T(2,128)S(1)}, u32[]{:S(2)}, u32[]{:S(2)}) async-start(f32[8,2,512]{2,1,0:T(2,128)} %reshape.191), calls=%async_computation | async-start | bytes 65536 | tf_op jit(solution)/shard_map/all_to_all | solution.py:422
  47.2 21.1 %copy-start.1 = (bf16[27,192,192]{2,1,0:T(8,128)(2,1)S(1)}, bf16[27,192,192]{2,1,0:T(8,128)(2,1)}, u32[]{:S(2)}) copy-start(bf16[27,192,192]{2,1,0:T(8,128)(2,1)} %weight_odd.1) | copy-start | bytes 5971972
  49.9 11.1 %collective-permute-start.1 = (bf16[384,512]{1,0:T(8,128)(2,1)}, bf16[384,512]{1,0:T(8,128)(2,1)}, u32[]{:S(2)}, u32[]{:S(2)}) collective-permute-start(bf16[384,512]{1,0:T(8,128)(2,1)} %pad_maximum_fusion.1.own), channel_id=1, source_target_pairs={{4,0},{8,4},{12,8},{16,12},{20,16},{24,20},{28,24},{5,1},{9,5},{13... | collective-permute-start | bytes 1179656 | tf_op jit(solution)/shard_map/ppermute | solution.py:433
  51.2 17.1 %collective-permute-start = (bf16[384,512]{1,0:T(8,128)(2,1)}, bf16[384,512]{1,0:T(8,128)(2,1)}, u32[]{:S(2)}, u32[]{:S(2)}) collective-permute-start(bf16[384,512]{1,0:T(8,128)(2,1)} %pad_maximum_fusion.1.own), channel_id=1, source_target_pairs={{0,4},{4,8},{8,12},{12,16},{16,20},{20,24},{24,28},{1,5},{5,9},{9,... | collective-permute-start | bytes 1179656 | tf_op jit(solution)/shard_map/ppermute | solution.py:432
  107.7 0.7 copy-start.7
  108.7 13.2 %copy-start.8 = (bf16[384,512]{1,0:T(8,128)(2,1)S(1)}, bf16[384,512]{1,0:T(8,128)(2,1)}, u32[]{:S(2)}) copy-start(bf16[384,512]{1,0:T(8,128)(2,1)} %copy-done.7) | copy-start | bytes 1179652
  131.0 2.0 %copy-start = (bf16[4608,384]{1,0:T(8,128)(2,1)S(1)}, bf16[4608,384]{1,0:T(8,128)(2,1)}, u32[]{:S(2)}) copy-start(bf16[4608,384]{1,0:T(8,128)(2,1)} %shard_map.105.x_ref) | copy-start | bytes 10616836
